TPU v7x, 512 devices: a whole 4x8x8 slice. The times are simulated.
512 devices in a mesh: row: 256 (over z, y, x), col: 2 (over core).
Axes of the slice: x: 4, y: 8, z: 8, core: 2. Of those that a mesh axis runs over, the one named last changes fastest.
Arguments:
- leaf_basis: float32 [4096, 128, 64], P(('row', 'col')), may hold values from -0.5 to 0.5
- local_transfer: bfloat16 [7168, 64, 64], P(('row', 'col')), may hold values from -0.5 to 0.5
- col_transfer: bfloat16 [256, 2, 64, 64], P('row'), may hold values from -0.5 to 0.5
- row_transfer: bfloat16 [256, 8, 64, 64], P('row'), as said below
- coupling: bfloat16 [122880, 64, 64], P(('row', 'col')), may hold values from -6 to 6
- slot_block_row: int32 [122880], P(('row', 'col')), may hold values from 0 to 7, as said below
- block_col: int32 [122880], P(('row', 'col')), may hold values from 0 to 47, as said below
- block_valid: int32 [122880], P(('row', 'col')), may hold values from 0 to 1, as said below
Outputs:
- projected: bfloat16 [122880, 64, 64], P(('row', 'col'))
- path_factor: float32 [512, 9, 64, 64], P(('row', 'col'))
Inputs may be any that keep to these rules, and one draw needn't show every extreme that they name: row_transfer[r, k] is the transfer of the ancestor k levels above row subtree r's cluster, so it is the same for all r with the same r // 2^k. `slot_block_row`: at each level, a device block's slots name each of its clusters of that level exactly 16 times. `block_col`: at each level, some slot of every device block names the first and some other slot the last of the listed clusters of that level. `block_valid`: at each level, a device block's real slots come first and are at least half of its slots of that level.
All inputs are finite; a program needn't handle non-finite values.
Results may differ from a plain program's by a relative error of at most 0.0015.
Values sent between devices are 32-bit elements; how exact they have to be, the bound alone decides.
A program may use at most 128 MiB of HBM per device.

v0:
```python
import jax
import jax.numpy as jnp
from jax import lax
from jax.sharding import PartitionSpec as P

HIGH = lax.Precision.HIGHEST


def from_partner(block, axis, distance):
    count = lax.axis_size(axis)
    route = []
    for low in range(count):
        high = low | 1 << distance
        if high != low and high < count:
            route += [(low, high), (high, low)]
    return lax.ppermute(block, axis, route)


def padded(cells, sides, width):
    for axis, dim in sides:
        count = lax.axis_size(axis)
        head = lax.slice_in_dim(cells, 0, width, axis=dim)
        tail = lax.slice_in_dim(cells, cells.shape[dim] - width, cells.shape[dim], axis=dim)
        cells = jnp.concatenate(
            [
                lax.ppermute(tail, axis, [(i, (i + 1) % count) for i in range(count)]),
                cells,
                lax.ppermute(head, axis, [((i + 1) % count, i) for i in range(count)]),
            ],
            axis=dim,
        )
    return cells


def upper_chol(stacked):
    gram_matrix = jnp.einsum("...mk,...ml->...kl", stacked, stacked, precision=HIGH)
    cholesky_lower = jnp.linalg.cholesky(gram_matrix)
    return jnp.swapaxes(cholesky_lower, -1, -2)


def merge_pairs(factors, transfers):
    scaled = jnp.einsum(
        "...nij,...njl->...nil", factors, transfers.astype(jnp.float32), precision=HIGH
    )
    extent = scaled.shape
    stacked = scaled.reshape(extent[:-3] + (extent[-3] // 2, 2 * extent[-2], extent[-1]))
    return upper_chol(stacked)


def project(rows_f, cols_f, blocks, valid_mask):
    left_product = jnp.einsum("bij,bjl->bil", rows_f, blocks.astype(jnp.float32), precision=HIGH)
    outcome = jnp.einsum("bil,bml->bim", left_product, cols_f, precision=HIGH)
    return jnp.where(valid_mask[:, None, None] == 1, outcome, 0.0).astype(jnp.bfloat16)


def pair_step(present_level, partner, position, height, table):
    upper_half = position // 2**height % 2
    lower_f = jnp.where(upper_half == 0, present_level, partner)
    higher_f = jnp.where(upper_half == 0, partner, present_level)
    return merge_pairs(jnp.stack([lower_f, higher_f]), table)[0]


def shards(
    leaf_basis,
    local_transfer,
    col_transfer,
    row_transfer,
    coupling,
    slot_block_row,
    block_col,
    block_valid,
):
    local_leaves = leaf_basis.shape[0]
    level_now = upper_chol(leaf_basis)
    factors = [level_now]
    offset = 0
    members = local_leaves
    while members > 1:
        level_now = merge_pairs(level_now, local_transfer[offset : offset + members])
        offset += members
        members //= 2
        factors.append(level_now)
    device_root = level_now[0]
    col_index = lax.axis_index("col")
    row_index = lax.axis_index("row")
    col_count = lax.axis_size("col")
    row_count = lax.axis_size("row")
    row_levels = row_count.bit_length() - 1
    col_table = col_transfer[0]
    row_path = row_transfer[0]
    parent_chain = []
    present_level = device_root
    offset = 0
    members = col_count
    height = 0
    partner = from_partner(present_level, "col", height)
    present_level = pair_step(present_level, partner, col_index, height, col_table)
    offset += members
    members //= 2
    parent_chain.append(present_level)
    for height in range(row_levels):
        scaled = jnp.einsum(
            "ij,jl->il", present_level, row_path[height].astype(jnp.float32), precision=HIGH
        )
        partner = from_partner(scaled, "row", height)
        upper_half = row_index // 2**height % 2
        lower_f = jnp.where(upper_half == 0, scaled, partner)
        higher_f = jnp.where(upper_half == 0, partner, scaled)
        present_level = upper_chol(jnp.concatenate([lower_f, higher_f], axis=0))
        parent_chain.append(present_level)
    path_factor = jnp.stack(parent_chain)[None]
    table_rows = 2 * local_leaves - 1
    per_cluster = coupling.shape[0] // table_rows
    pieces = []
    leading_slot = 0
    for height in range(len(factors)):
        level_table = factors[height]
        slots = per_cluster * level_table.shape[0]
        gathered = lax.all_gather(level_table, "col", axis=0, tiled=True)
        rim_table = padded(gathered[None], (("row", 0),), 1)
        neighbours = rim_table.reshape((-1,) + gathered.shape[1:])
        rows_f = jnp.take(level_table, slot_block_row[leading_slot : leading_slot + slots], axis=0)
        cols_f = jnp.take(neighbours, block_col[leading_slot : leading_slot + slots], axis=0)
        pieces.append(
            project(
                rows_f,
                cols_f,
                coupling[leading_slot : leading_slot + slots],
                block_valid[leading_slot : leading_slot + slots],
            )
        )
        leading_slot += slots
    projected = jnp.concatenate(pieces, axis=0)
    return (projected, path_factor)


def solution(mesh):
    placed = (
        P(("row", "col"), None, None),
        P(("row", "col"), None, None),
        P("row", None, None, None),
        P("row", None, None, None),
        P(("row", "col"), None, None),
        P(("row", "col")),
        P(("row", "col")),
        P(("row", "col")),
    )
    return jax.shard_map(
        shards,
        mesh=mesh,
        in_specs=placed,
        out_specs=(P(("row", "col"), None, None), P(("row", "col"), None, None, None)),
        check_vma=False,
    )
```

profile of v0, /device:TPU:6, one launch (start us, length us, event | category | flops | bytes accessed | tf_op | source)
XLA Modules:
  0.0 362.4 jit_solution(5187582844714935258)
XLA Ops:
  2.3 46.9 %custom-call.17 = f32[8,64,64]{2,1,0:T(8,128)S(1)} custom-call(f32[8,64,64]{2,1,0:T(8,128)S(1)} %fusion.32), custom_call_target="Cholesky" | custom-call | tf_op jit(solution)/shard_map/jit(cholesky)/cholesky | solution.py:37
  50.6 23.5 %custom-call.18 = f32[4,64,64]{2,1,0:T(8,128)S(1)} custom-call(f32[4,64,64]{2,1,0:T(8,128)S(1)} %fusion.40), custom_call_target="Cholesky" | custom-call | tf_op jit(solution)/shard_map/jit(cholesky)/cholesky | solution.py:37
  75.1 11.7 %custom-call.19 = f32[2,64,64]{2,1,0:T(8,128)S(1)} custom-call(f32[2,64,64]{2,1,0:T(8,128)S(1)} %fusion.52), custom_call_target="Cholesky" | custom-call | tf_op jit(solution)/shard_map/jit(cholesky)/cholesky | solution.py:37
  87.6 5.8 %custom-call.21 = f32[1,64,64]{2,1,0:T(8,128)S(1)} custom-call(f32[1,64,64]{2,1,0:T(8,128)S(1)} %fusion.95), custom_call_target="Cholesky" | custom-call | tf_op jit(solution)/shard_map/jit(cholesky)/cholesky | solution.py:37
  96.9 2.7 collective-permute-start.7
  99.6 5.2 %collective-permute-start.6 = (f32[1,2,64,64]{3,2,1,0:T(8,128)}, f32[1,2,64,64]{3,2,1,0:T(8,128)}, u32[]{:S(2)}, u32[]{:S(2)}) collective-permute-start(f32[1,2,64,64]{3,2,1,0:T(8,128)} %bitcast.19), channel_id=1, source_target_pairs={{0,2},{2,4},{4,6},{6,8},{8,10},{10,12},{12,14},{14,16},{16,18},{18... | collective-permute-start | bytes 98312 | tf_op jit(solution)/shard_map/ppermute | solution.py:26
  105.0 2.0 all_gather.14
  109.0 6.0 %collective-permute-start.4 = (f32[1,4,64,64]{3,2,1,0:T(8,128)}, f32[1,4,64,64]{3,2,1,0:T(8,128)}, u32[]{:S(2)}, u32[]{:S(2)}) collective-permute-start(f32[1,4,64,64]{3,2,1,0:T(8,128)} %bitcast.12), channel_id=1, source_target_pairs={{0,2},{2,4},{4,6},{6,8},{8,10},{10,12},{12,14},{14,16},{16,18},{18... | collective-permute-start | bytes 196616 | tf_op jit(solution)/shard_map/ppermute | solution.py:26
  115.0 2.4 collective-permute-start.8
  125.8 2.4 copy.224
  128.3 2.2 copy.223
  131.1 2.4 copy.222
  133.6 2.0 gather_fusion.2
  135.6 3.8 %copy.221 = bf16[128,64,64]{2,1,0:T(8,128)(2,1)} copy(bf16[128,64,64]{0,2,1:T(8,128)(2,1)S(1)} %slice-done.1) | data formatting | bytes 2097152
  139.6 2.7 gather_fusion
  142.4 2.6 all_gather.12
  145.5 2.1 fusion.19
  149.7 5.4 %fusion.2 = f32[128,64,64]{2,1,0:T(8,128)} fusion(bf16[128,64,64]{2,1,0:T(8,128)(2,1)S(1)} %copy-done.4, f32[128,64,64]{1,2,0:T(8,128)S(1)} %copy-done.1, pred[128]{0:T(512)(128)(4,1)S(1)} %copy-done.27), kind=kOutput, calls=%fused_computation.10 | convolution fusion | flops 403177472 | bytes 5243008 | tf_op jit(solution)/shard_map/bij,bjl->bil/dot_general | solution.py:51
  155.1 2.3 all_gather.13
  158.9 5.8 %custom-call.22 = f32[1,64,64]{2,1,0:T(8,128)S(1)} custom-call(f32[1,64,64]{2,1,0:T(8,128)S(1)} %fusion.94), custom_call_target="Cholesky" | custom-call | tf_op jit(solution)/shard_map/jit(cholesky)/cholesky | solution.py:37
  170.2 2.6 collective-permute-done.9
  175.1 5.8 %cholesky.310 = f32[64,64]{1,0:T(8,128)S(1)} custom-call(f32[64,64]{1,0:T(8,128)S(1)} %fusion.103), custom_call_target="Cholesky" | custom-call | tf_op jit(solution)/shard_map/jit(cholesky)/cholesky | solution.py:37
  183.3 6.0 %collective-permute-start.2 = (f32[1,8,64,64]{3,2,1,0:T(8,128)}, f32[1,8,64,64]{3,2,1,0:T(8,128)}, u32[]{:S(2)}, u32[]{:S(2)}) collective-permute-start(f32[1,8,64,64]{3,2,1,0:T(8,128)} %bitcast.7), channel_id=1, source_target_pairs={{0,2},{2,4},{4,6},{6,8},{8,10},{10,12},{12,14},{14,16},{16,18},{18... | collective-permute-start | bytes 393224 | tf_op jit(solution)/shard_map/ppermute | solution.py:26
  189.3 13.1 %collective-permute-start.10 = (f32[64,64]{0,1:T(8,128)S(1)}, f32[64,64]{0,1:T(8,128)}, u32[]{:S(2)}, u32[]{:S(2)}) collective-permute-start(f32[64,64]{0,1:T(8,128)S(1)} %fusion.112), channel_id=1, source_target_pairs={{0,4},{4,0},{2,6},{6,2},{8,12},{12,8},{10,14},{14,10},{16,20},{20,... | collective-permute-start | bytes 49160 | tf_op jit(solution)/shard_map/ppermute | solution.py:16
  204.7 2.1 fusion.17
  208.0 8.7 %collective-permute-start.1 = (f32[1,16,64,64]{3,2,1,0:T(8,128)}, f32[1,16,64,64]{3,2,1,0:T(8,128)}, u32[]{:S(2)}, u32[]{:S(2)}) collective-permute-start(f32[1,16,64,64]{3,2,1,0:T(8,128)} %bitcast.172), channel_id=1, source_target_pairs={{2,0},{4,2},{6,4},{8,6},{10,8},{12,10},{14,12},{16,14},{18,16},{20... | collective-permute-start | bytes 786440 | tf_op jit(solution)/shard_map/ppermute | solution.py:28
  217.9 5.8 %cholesky.321 = f32[64,64]{1,0:T(8,128)S(1)} custom-call(f32[64,64]{1,0:T(8,128)S(1)} %fusion.102), custom_call_target="Cholesky" | custom-call | tf_op jit(solution)/shard_map/jit(cholesky)/cholesky | solution.py:37
  233.1 2.5 copy.178
  235.6 3.7 %collective-permute-done.11 = f32[64,64]{0,1:T(8,128)S(1)} collective-permute-done((f32[64,64]{0,1:T(8,128)S(1)}, f32[64,64]{0,1:T(8,128)S(1)}, u32[]{:S(2)}, u32[]{:S(2)}) %collective-permute-start.11) | collective-permute-done | bytes 16416 | tf_op jit(solution)/shard_map/ppermute | solution.py:16
  239.7 5.8 %cholesky.332 = f32[64,64]{1,0:T(8,128)S(1)} custom-call(f32[64,64]{1,0:T(8,128)S(1)} %fusion.101), custom_call_target="Cholesky" | custom-call | tf_op jit(solution)/shard_map/jit(cholesky)/cholesky | solution.py:37
  249.0 3.6 fusion.16
  254.3 5.8 %cholesky.343 = f32[64,64]{1,0:T(8,128)S(1)} custom-call(f32[64,64]{1,0:T(8,128)S(1)} %fusion.100), custom_call_target="Cholesky" | custom-call | tf_op jit(solution)/shard_map/jit(cholesky)/cholesky | solution.py:37
  264.9 6.9 %collective-permute-done.13 = f32[64,64]{0,1:T(8,128)S(1)} collective-permute-done((f32[64,64]{0,1:T(8,128)S(1)}, f32[64,64]{0,1:T(8,128)S(1)}, u32[]{:S(2)}, u32[]{:S(2)}) %collective-permute-start.13) | collective-permute-done | bytes 16416 | tf_op jit(solution)/shard_map/ppermute | solution.py:16
  272.1 5.8 %cholesky.354 = f32[64,64]{1,0:T(8,128)S(1)} custom-call(f32[64,64]{1,0:T(8,128)S(1)} %fusion.99), custom_call_target="Cholesky" | custom-call | tf_op jit(solution)/shard_map/jit(cholesky)/cholesky | solution.py:37
  282.7 2.6 collective-permute-done.14
  285.7 5.8 %cholesky.365 = f32[64,64]{1,0:T(8,128)S(1)} custom-call(f32[64,64]{1,0:T(8,128)S(1)} %fusion.98), custom_call_target="Cholesky" | custom-call | tf_op jit(solution)/shard_map/jit(cholesky)/cholesky | solution.py:37
  293.7 3.3 collective-permute-start.15
  299.4 2.0 gather_fusion.3
  301.4 2.9 copy.169
  305.5 5.8 %cholesky.376 = f32[64,64]{1,0:T(8,128)S(1)} custom-call(f32[64,64]{1,0:T(8,128)S(1)} %fusion.97), custom_call_target="Cholesky" | custom-call | tf_op jit(solution)/shard_map/jit(cholesky)/cholesky | solution.py:37
  312.9 8.4 %collective-permute-start.16 = (f32[64,64]{0,1:T(8,128)S(1)}, f32[64,64]{0,1:T(8,128)S(1)}, u32[]{:S(2)}, u32[]{:S(2)}) collective-permute-start(f32[64,64]{0,1:T(8,128)S(1)} %fusion.118), channel_id=1, source_target_pairs={{0,256},{256,0},{2,258},{258,2},{4,260},{260,4},{6,262},{262,6},{8... | collective-permute-start | bytes 49160 | tf_op jit(solution)/shard_map/ppermute | solution.py:16
  321.4 5.0 %select_convert_fusion.1 = bf16[64,64,64]{2,1,0:T(8,128)(2,1)} fusion(f32[64,64,64]{2,1,0:T(8,128)S(1)} %fusion.6, f32[64,64,64]{1,2,0:T(8,128)} %copy.169, pred[64]{0:T(512)(128)(4,1)S(1)} %copy-done.17, pred[64]{0:T(512)(128)(4,1)S(1)} %copy-done.18), kind=kOutput, calls=%fused_computation.13 | convolution fusion | flops 202113024 | bytes 2621568 | tf_op jit(solution)/shard_map/bil,bml->bim/dot_general | solution.py:52
  327.4 5.8 %cholesky.387 = f32[64,64]{1,0:T(8,128)S(1)} custom-call(f32[64,64]{1,0:T(8,128)S(1)} %fusion.96), custom_call_target="Cholesky" | custom-call | tf_op jit(solution)/shard_map/jit(cholesky)/cholesky | solution.py:37
  336.9 2.8 gather_fusion.1
  339.7 5.7 %copy.160 = f32[128,64,64]{1,2,0:T(8,128)} copy(f32[128,64,64]{2,1,0:T(8,128)} %gather_fusion.1) | data formatting | bytes 4194304 | tf_op jit(solution)/shard_map/jit(_take)/gather | solution.py:123
  345.4 8.5 %select_convert_fusion = bf16[128,64,64]{2,1,0:T(8,128)(2,1)S(1)} fusion(pred[128]{0:T(512)(128)(4,1)S(1)} %copy-done.16, f32[128,64,64]{2,1,0:T(8,128)} %fusion.2, f32[128,64,64]{1,2,0:T(8,128)} %copy.160, pred[128]{0:T(512)(128)(4,1)S(1)} %copy-done.15), kind=kOutput, calls=%fused_computation.7 | convolution fusion | flops 404226048 | bytes 5243136 | tf_op jit(solution)/shard_map/bil,bml->bim/dot_general | solution.py:52
  354.0 2.5 pad_maximum_fusion
  356.5 5.7 %copy.199 = bf16[240,64,64]{0,2,1:T(8,128)(2,1)} copy(bf16[240,64,64]{2,1,0:T(8,128)(2,1)} %pad_maximum_fusion) | data formatting | bytes 3932160
  (217 shorter events, 74.9 us)
Async XLA Ops:
  0.6 1.0 copy-start
  0.6 48.7 %copy-start.10 = (bf16[14,64,64]{2,1,0:T(8,128)(2,1)S(1)}, bf16[14,64,64]{2,1,0:T(8,128)(2,1)}, u32[]{:S(2)}) copy-start(bf16[14,64,64]{2,1,0:T(8,128)(2,1)} %param.11) | copy-start | bytes 344068
  49.8 67.6 %copy-start.2 = (bf16[240,64,64]{0,2,1:T(8,128)(2,1)S(1)}, bf16[240,64,64]{0,2,1:T(8,128)(2,1)}, u32[]{:S(2)}) copy-start(bf16[240,64,64]{0,2,1:T(8,128)(2,1)} %param.14) | copy-start | bytes 5898244
  96.9 86.4 %collective-permute-start.7 = (f32[1,2,64,64]{3,2,1,0:T(8,128)}, f32[1,2,64,64]{3,2,1,0:T(8,128)}, u32[]{:S(2)}, u32[]{:S(2)}) collective-permute-start(f32[1,2,64,64]{3,2,1,0:T(8,128)} %bitcast.19), channel_id=1, source_target_pairs={{2,0},{4,2},{6,4},{8,6},{10,8},{12,10},{14,12},{16,14},{18,16},{20... | collective-permute-start | bytes 98312 | tf_op jit(solution)/shard_map/ppermute | solution.py:28
  99.6 89.7 %collective-permute-start.6 = (f32[1,2,64,64]{3,2,1,0:T(8,128)}, f32[1,2,64,64]{3,2,1,0:T(8,128)}, u32[]{:S(2)}, u32[]{:S(2)}) collective-permute-start(f32[1,2,64,64]{3,2,1,0:T(8,128)} %bitcast.19), channel_id=1, source_target_pairs={{0,2},{2,4},{4,6},{6,8},{8,10},{10,12},{12,14},{14,16},{16,18},{18... | collective-permute-start | bytes 98312 | tf_op jit(solution)/shard_map/ppermute | solution.py:26
  107.0 119.5 %collective-permute-start.5 = (f32[1,4,64,64]{3,2,1,0:T(8,128)}, f32[1,4,64,64]{3,2,1,0:T(8,128)}, u32[]{:S(2)}, u32[]{:S(2)}) collective-permute-start(f32[1,4,64,64]{3,2,1,0:T(8,128)} %bitcast.12), channel_id=1, source_target_pairs={{2,0},{4,2},{6,4},{8,6},{10,8},{12,10},{14,12},{16,14},{18,16},{20... | collective-permute-start | bytes 196616 | tf_op jit(solution)/shard_map/ppermute | solution.py:28
  109.0 119.5 %collective-permute-start.4 = (f32[1,4,64,64]{3,2,1,0:T(8,128)}, f32[1,4,64,64]{3,2,1,0:T(8,128)}, u32[]{:S(2)}, u32[]{:S(2)}) collective-permute-start(f32[1,4,64,64]{3,2,1,0:T(8,128)} %bitcast.12), channel_id=1, source_target_pairs={{0,2},{2,4},{4,6},{6,8},{8,10},{10,12},{12,14},{14,16},{16,18},{18... | collective-permute-start | bytes 196616 | tf_op jit(solution)/shard_map/ppermute | solution.py:26
  115.0 42.5 %collective-permute-start.8 = (f32[64,64]{0,1:T(8,128)S(1)}, f32[64,64]{0,1:T(8,128)}, u32[]{:S(2)}, u32[]{:S(2)}) collective-permute-start(f32[64,64]{0,1:T(8,128)S(1)} %get-tuple-element.47), channel_id=1, source_target_pairs={{0,1},{1,0},{2,3},{3,2},{4,5},{5,4},{6,7},{7,6},{8,9},{9,8},{10,11... | collective-permute-start | bytes 49160 | tf_op jit(solution)/shard_map/ppermute | solution.py:16
  117.5 2.8 copy-start.28
  117.5 4.6 %copy-start.13 = (s32[240]{0:T(256)S(1)}, s32[240]{0:T(256)}, u32[]{:S(2)}) copy-start(s32[240]{0:T(256)} %param.16) | copy-start | bytes 2884
  117.5 5.2 %copy-start.14 = (s32[240]{0:T(256)S(1)}, s32[240]{0:T(256)}, u32[]{:S(2)}) copy-start(s32[240]{0:T(256)} %param.17) | copy-start | bytes 2884
  128.3 2.8 slice-start
  133.6 2.0 copy-start.22
  133.6 2.0 slice-start.1
  135.6 3.8 %copy-start.23 = (s32[128]{0:T(128)S(1)}, s32[128]{0:T(128)}, u32[]{:S(2)}) copy-start(s32[128]{0:T(128)} %get-tuple-element.17) | copy-start | bytes 1540
  139.6 5.4 %copy-start.21 = (s32[128]{0:T(128)S(1)}, s32[128]{0:T(128)}, u32[]{:S(2)}) copy-start(s32[128]{0:T(128)} %get-tuple-element.15) | copy-start | bytes 1540
  139.6 5.4 %copy-start.8 = (bf16[16,64,64]{2,1,0:T(8,128)(2,1)S(1)}, bf16[16,64,64]{2,1,0:T(8,128)(2,1)}, u32[]{:S(2)}) copy-start(bf16[16,64,64]{2,1,0:T(8,128)(2,1)} %copy.224) | copy-start | bytes 393220
  139.6 5.4 %copy-start.24 = (pred[16]{0:T(512)(128)(4,1)S(1)}, pred[16]{0:T(512)(128)(4,1)}, u32[]{:S(2)}) copy-start(pred[16]{0:T(512)(128)(4,1)} %compare_and_fusion.1) | copy-start | bytes 52
  139.6 5.8 %copy-start.25 = (pred[32]{0:T(512)(128)(4,1)S(1)}, pred[32]{0:T(512)(128)(4,1)}, u32[]{:S(2)}) copy-start(pred[32]{0:T(512)(128)(4,1)} %get-tuple-element.24) | copy-start | bytes 100
  142.4 5.2 %copy-start.3 = (f32[64,64,64]{1,2,0:T(8,128)S(1)}, f32[64,64,64]{1,2,0:T(8,128)}, u32[]{:S(2)}) copy-start(f32[64,64,64]{1,2,0:T(8,128)} %gather_fusion.2) | copy-start | bytes 3145732
  142.4 5.2 %copy-start.6 = (bf16[64,64,64]{2,1,0:T(8,128)(2,1)S(1)}, bf16[64,64,64]{2,1,0:T(8,128)(2,1)}, u32[]{:S(2)}) copy-start(bf16[64,64,64]{2,1,0:T(8,128)(2,1)} %copy.222) | copy-start | bytes 1572868
  142.4 5.2 %copy-start.26 = (pred[64]{0:T(512)(128)(4,1)S(1)}, pred[64]{0:T(512)(128)(4,1)}, u32[]{:S(2)}) copy-start(pred[64]{0:T(512)(128)(4,1)} %get-tuple-element.20) | copy-start | bytes 196
  145.4 4.1 %copy-start.4 = (bf16[128,64,64]{2,1,0:T(8,128)(2,1)S(1)}, bf16[128,64,64]{2,1,0:T(8,128)(2,1)}, u32[]{:S(2)}) copy-start(bf16[128,64,64]{2,1,0:T(8,128)(2,1)} %copy.221) | copy-start | bytes 3145732
  147.5 2.2 copy-start.1
  147.5 2.2 copy-start.27
  149.7 8.5 %copy-start.12 = (bf16[1,2,64,64]{3,2,1,0:T(8,128)(2,1)S(1)}, bf16[1,2,64,64]{3,2,1,0:T(8,128)(2,1)}, u32[]{:S(2)}) copy-start(bf16[1,2,64,64]{3,2,1,0:T(8,128)(2,1)} %param.12) | copy-start | bytes 49156
  158.8 65.6 %copy-start.11 = (bf16[1,8,64,64]{3,2,1,0:T(8,128)(2,1)S(1)}, bf16[1,8,64,64]{3,2,1,0:T(8,128)(2,1)}, u32[]{:S(2)}) copy-start(bf16[1,8,64,64]{3,2,1,0:T(8,128)(2,1)} %param.13) | copy-start | bytes 196612
  167.0 5.8 %collective-permute-start.9 = (f32[64,64]{0,1:T(8,128)S(1)}, f32[64,64]{0,1:T(8,128)S(1)}, u32[]{:S(2)}, u32[]{:S(2)}) collective-permute-start(f32[64,64]{0,1:T(8,128)S(1)} %fusion.92), channel_id=1, source_target_pairs={{0,2},{2,0},{4,6},{6,4},{8,10},{10,8},{12,14},{14,12},{16,18},{18,... | collective-permute-start | bytes 49160 | tf_op jit(solution)/shard_map/ppermute | solution.py:16
  172.8 125.4 %collective-permute-start.3 = (f32[1,8,64,64]{3,2,1,0:T(8,128)}, f32[1,8,64,64]{3,2,1,0:T(8,128)}, u32[]{:S(2)}, u32[]{:S(2)}) collective-permute-start(f32[1,8,64,64]{3,2,1,0:T(8,128)} %bitcast.7), channel_id=1, source_target_pairs={{2,0},{4,2},{6,4},{8,6},{10,8},{12,10},{14,12},{16,14},{18,16},{20... | collective-permute-start | bytes 393224 | tf_op jit(solution)/shard_map/ppermute | solution.py:28
  183.3 115.0 %collective-permute-start.2 = (f32[1,8,64,64]{3,2,1,0:T(8,128)}, f32[1,8,64,64]{3,2,1,0:T(8,128)}, u32[]{:S(2)}, u32[]{:S(2)}) collective-permute-start(f32[1,8,64,64]{3,2,1,0:T(8,128)} %bitcast.7), channel_id=1, source_target_pairs={{0,2},{2,4},{4,6},{6,8},{8,10},{10,12},{12,14},{14,16},{16,18},{18... | collective-permute-start | bytes 393224 | tf_op jit(solution)/shard_map/ppermute | solution.py:26
  189.3 18.7 %collective-permute-start.10 = (f32[64,64]{0,1:T(8,128)S(1)}, f32[64,64]{0,1:T(8,128)}, u32[]{:S(2)}, u32[]{:S(2)}) collective-permute-start(f32[64,64]{0,1:T(8,128)S(1)} %fusion.112), channel_id=1, source_target_pairs={{0,4},{4,0},{2,6},{6,2},{8,12},{12,8},{10,14},{14,10},{16,20},{20,... | collective-permute-start | bytes 49160 | tf_op jit(solution)/shard_map/ppermute | solution.py:16
  208.0 127.4 %collective-permute-start.1 = (f32[1,16,64,64]{3,2,1,0:T(8,128)}, f32[1,16,64,64]{3,2,1,0:T(8,128)}, u32[]{:S(2)}, u32[]{:S(2)}) collective-permute-start(f32[1,16,64,64]{3,2,1,0:T(8,128)} %bitcast.172), channel_id=1, source_target_pairs={{2,0},{4,2},{6,4},{8,6},{10,8},{12,10},{14,12},{16,14},{18,16},{20... | collective-permute-start | bytes 786440 | tf_op jit(solution)/shard_map/ppermute | solution.py:28
  226.5 108.9 %collective-permute-start = (f32[1,16,64,64]{3,2,1,0:T(8,128)}, f32[1,16,64,64]{3,2,1,0:T(8,128)}, u32[]{:S(2)}, u32[]{:S(2)}) collective-permute-start(f32[1,16,64,64]{3,2,1,0:T(8,128)} %bitcast.173), channel_id=1, source_target_pairs={{0,2},{2,4},{4,6},{6,8},{8,10},{10,12},{12,14},{14,16},{16,18},{18... | collective-permute-start | bytes 786440 | tf_op jit(solution)/shard_map/ppermute | solution.py:26
  228.5 10.9 %collective-permute-start.11 = (f32[64,64]{0,1:T(8,128)S(1)}, f32[64,64]{0,1:T(8,128)S(1)}, u32[]{:S(2)}, u32[]{:S(2)}) collective-permute-start(f32[64,64]{0,1:T(8,128)S(1)} %fusion.113), channel_id=1, source_target_pairs={{0,8},{8,0},{2,10},{10,2},{4,12},{12,4},{6,14},{14,6},{16,24},{24,... | collective-permute-start | bytes 49160 | tf_op jit(solution)/shard_map/ppermute | solution.py:16
  231.4 17.6 %copy-start.19 = (pred[32]{0:T(512)(128)(4,1)S(1)}, pred[32]{0:T(512)(128)(4,1)}, u32[]{:S(2)}) copy-start(pred[32]{0:T(512)(128)(4,1)} %get-tuple-element.22) | copy-start | bytes 100
  231.5 17.6 %copy-start.20 = (pred[32]{0:T(512)(128)(4,1)S(1)}, pred[32]{0:T(512)(128)(4,1)}, u32[]{:S(2)}) copy-start(pred[32]{0:T(512)(128)(4,1)} %get-tuple-element.50) | copy-start | bytes 100
  247.1 6.8 %collective-permute-start.12 = (f32[64,64]{0,1:T(8,128)S(1)}, f32[64,64]{0,1:T(8,128)S(1)}, u32[]{:S(2)}, u32[]{:S(2)}) collective-permute-start(f32[64,64]{0,1:T(8,128)S(1)} %fusion.114), channel_id=1, source_target_pairs={{0,16},{16,0},{2,18},{18,2},{4,20},{20,4},{6,22},{22,6},{8,24},{24... | collective-permute-start | bytes 49160 | tf_op jit(solution)/shard_map/ppermute | solution.py:16
  261.7 10.1 %collective-permute-start.13 = (f32[64,64]{0,1:T(8,128)S(1)}, f32[64,64]{0,1:T(8,128)S(1)}, u32[]{:S(2)}, u32[]{:S(2)}) collective-permute-start(f32[64,64]{0,1:T(8,128)S(1)} %fusion.115), channel_id=1, source_target_pairs={{0,32},{32,0},{2,34},{34,2},{4,36},{36,4},{6,38},{38,6},{8,40},{40... | collective-permute-start | bytes 49160 | tf_op jit(solution)/shard_map/ppermute | solution.py:16
  279.5 5.8 %collective-permute-start.14 = (f32[64,64]{0,1:T(8,128)S(1)}, f32[64,64]{0,1:T(8,128)S(1)}, u32[]{:S(2)}, u32[]{:S(2)}) collective-permute-start(f32[64,64]{0,1:T(8,128)S(1)} %fusion.116), channel_id=1, source_target_pairs={{0,64},{64,0},{2,66},{66,2},{4,68},{68,4},{6,70},{70,6},{8,72},{72... | collective-permute-start | bytes 49160 | tf_op jit(solution)/shard_map/ppermute | solution.py:16
  293.7 10.7 %collective-permute-start.15 = (f32[64,64]{0,1:T(8,128)}, f32[64,64]{0,1:T(8,128)}, u32[]{:S(2)}, u32[]{:S(2)}) collective-permute-start(f32[64,64]{0,1:T(8,128)} %fusion.117), channel_id=1, source_target_pairs={{0,128},{128,0},{2,130},{130,2},{4,132},{132,4},{6,134},{134,6},{8... | collective-permute-start | bytes 49160 | tf_op jit(solution)/shard_map/ppermute | solution.py:16
  301.4 19.9 %copy-start.17 = (pred[64]{0:T(512)(128)(4,1)S(1)}, pred[64]{0:T(512)(128)(4,1)}, u32[]{:S(2)}) copy-start(pred[64]{0:T(512)(128)(4,1)} %get-tuple-element.18) | copy-start | bytes 196
  301.4 19.9 %copy-start.18 = (pred[64]{0:T(512)(128)(4,1)S(1)}, pred[64]{0:T(512)(128)(4,1)}, u32[]{:S(2)}) copy-start(pred[64]{0:T(512)(128)(4,1)} %get-tuple-element.51) | copy-start | bytes 196
  312.9 14.1 %collective-permute-start.16 = (f32[64,64]{0,1:T(8,128)S(1)}, f32[64,64]{0,1:T(8,128)S(1)}, u32[]{:S(2)}, u32[]{:S(2)}) collective-permute-start(f32[64,64]{0,1:T(8,128)S(1)} %fusion.118), channel_id=1, source_target_pairs={{0,256},{256,0},{2,258},{258,2},{4,260},{260,4},{6,262},{262,6},{8... | collective-permute-start | bytes 49160 | tf_op jit(solution)/shard_map/ppermute | solution.py:16
  321.4 5.0 %copy-start.9 = (f32[9,64,64]{1,2,0:T(8,128)S(1)}, f32[9,64,64]{1,2,0:T(8,128)}, u32[]{:S(2)}) copy-start(f32[9,64,64]{1,2,0:T(8,128)} %bitcast_dynamic-update-slice_fusion.2) | copy-start | bytes 442372
  339.7 5.7 %copy-start.15 = (pred[128]{0:T(512)(128)(4,1)S(1)}, pred[128]{0:T(512)(128)(4,1)}, u32[]{:S(2)}) copy-start(pred[128]{0:T(512)(128)(4,1)} %get-tuple-element.14) | copy-start | bytes 388
  339.7 5.7 %copy-start.16 = (pred[128]{0:T(512)(128)(4,1)S(1)}, pred[128]{0:T(512)(128)(4,1)}, u32[]{:S(2)}) copy-start(pred[128]{0:T(512)(128)(4,1)} %get-tuple-element.52) | copy-start | bytes 388
  345.4 8.6 %copy-start.5 = (bf16[64,64,64]{2,1,0:T(8,128)(2,1)S(1)}, bf16[64,64,64]{2,1,0:T(8,128)(2,1)}, u32[]{:S(2)}) copy-start(bf16[64,64,64]{2,1,0:T(8,128)(2,1)} %select_convert_fusion.1) | copy-start | bytes 1572868
  345.4 8.6 %copy-start.7 = (bf16[32,64,64]{2,1,0:T(8,128)(2,1)S(1)}, bf16[32,64,64]{2,1,0:T(8,128)(2,1)}, u32[]{:S(2)}) copy-start(bf16[32,64,64]{2,1,0:T(8,128)(2,1)} %fusion.16) | copy-start | bytes 786436
where the time goes:
time: 370 us; the launch traced here: 362 us
  other arithmetic  174 us (47%)
  starting transfers between devices  71.3 us (19%)
  local copies, waits for them, and re-layouts  47.1 us (13%)
  matrix products  43.4 us (12%)
  waiting for transfers between devices  15.9 us (4%)
  blocking collectives  8.87 us (2%)
    another operation x40, other arithmetic, upper_chol(): cholesky_lower = jnp.linalg.cholesky(gram_matrix)  148 us
    ppermute x9, starting transfers between devices, from_partner(): return lax.ppermute(block, axis, route)  36.8 us
    dot_general x4, matrix products, project(): outcome = jnp.einsum('bil,bml->bim', left_product, cols_f, precision=HIGH)  19.2 us
    ppermute x4, starting transfers between devices, padded(): lax.ppermute(tail, axis, [(i, (i + 1) % count) for i in range(count)])  19.2 us
    gather x7, local copies, waits for them, and re-layouts, shards(): jnp.take(neighbours, block_col[leading_slot:leading_slot + slots], axis=0)  18.9 us
    unnamed x64, local copies, waits for them, and re-layouts  18.6 us
    ppermute x9, waiting for transfers between devices, from_partner(): return lax.ppermute(block, axis, route)  15.9 us
    ppermute x4, starting transfers between devices, padded(): lax.ppermute(head, axis, [((i + 1) % count, i) for i in range(count)])  15.3 us
  transfers between devices with their start and end apart: 17, of which 4 were waited for; matrix products, arithmetic and copies ran while one was open for 40% of the time, Pallas kernels for 0%

commit v1 on v0

v1 whole, which is shorter than its diff:
```python
import functools

import jax
import jax.numpy as jnp
from jax import lax
from jax.experimental import pallas as pl
from jax.experimental.pallas import tpu as pltpu
from jax.sharding import PartitionSpec as P

BF = jnp.bfloat16
F32 = jnp.float32
NT = (((1,), (1,)), ((), ()))
MESH = pl.DeviceIdType.MESH
VMEM = pl.BlockSpec(memory_space=pltpu.VMEM)
SMEM = pl.BlockSpec(memory_space=pltpu.SMEM)

LEVELS = ((0, 128, 3, 0), (128, 64, 2, 8), (192, 32, 1, 12), (224, 16, 0, 14))
ROUNDS = ((0, 2), (2, 5), (5, 8))
ENTRIES = 16


def split2(x):
    high = x.astype(BF)
    return high, (x - high.astype(F32)).astype(BF)


def split3(x):
    high = x.astype(BF)
    rest = x - high.astype(F32)
    middle = rest.astype(BF)
    return high, middle, (rest - middle.astype(F32)).astype(BF)


def gram(xt):
    h, m, l = split3(xt)
    left = jnp.concatenate([h, h, m, h, l, m], axis=1)
    right = jnp.concatenate([h, m, h, l, h, m], axis=1)
    return lax.dot_general(left, right, NT, preferred_element_type=F32)


def tripled(transfer):
    et = transfer.astype(F32).T.astype(BF)
    return jnp.concatenate([et, et, et], axis=1)


def sandwich(et3, g):
    y = lax.dot_general(et3, jnp.concatenate(split3(g), axis=1), NT, preferred_element_type=F32)
    return lax.dot_general(jnp.concatenate(split3(y), axis=1), et3, NT, preferred_element_type=F32)


def folded(g):
    return jnp.concatenate([g[:32], g[32:]], axis=1)


def unfolded(g):
    return jnp.concatenate([g[:, :64], g[:, 64:]], axis=0)


def pick(row, lane):
    lanes = lax.broadcasted_iota(jnp.int32, row.shape, 1)
    index = jnp.where(lanes < 64, lane, 64 + lane)
    return jnp.take_along_axis(row, index, axis=1, mode="promise_in_bounds")


def chol_pack(a_ref, u_ref, size=64, width=8):
    column = lax.broadcasted_iota(jnp.int32, (8, 128), 1) % 64
    for first in range(0, size, width):
        rows = [a_ref[first + i] for i in range(width)]
        for m in range(first):
            done = u_ref[m]
            for i in range(width):
                rows[i] = rows[i] - pick(done, first + i) * done
        entry = {}
        for i in range(width):
            for j in range(i, width):
                entry[i, j] = pick(rows[i], first + j)
        for k in range(width):
            scale = lax.rsqrt(entry[k, k])
            top = rows[k] * scale
            u_ref[first + k] = jnp.where(column < first + k, 0.0, top)
            factor = {j: entry[k, j] * scale for j in range(k + 1, width)}
            for i in range(k + 1, width):
                rows[i] = rows[i] - factor[i] * top
                for j in range(i, width):
                    entry[i, j] = entry[i, j] - factor[i] * factor[j]


def local_kernel(leaf_ref, transfer_ref, u_ref, root_ref, a_ref, et_ref):
    for i in range(14):
        et_ref[i] = tripled(transfer_ref[i])
    level = [gram(leaf_ref[i]) for i in range(8)]
    grams = list(level)
    offset = 0
    while len(level) > 1:
        parts = [sandwich(et_ref[offset + i], g) for i, g in enumerate(level)]
        offset += len(level)
        level = [parts[i] + parts[i + 1] for i in range(0, len(parts), 2)]
        grams += level
    root_ref[...] = level[0]
    row = lax.broadcasted_iota(jnp.int32, (64, 64), 0)
    column = lax.broadcasted_iota(jnp.int32, (64, 64), 1)
    grams.append(jnp.where(row == column, 1.0, 0.0))
    for b in range(8):
        a_ref[:, b, :] = jnp.concatenate([grams[b], grams[8 + b]], axis=1)
    chol_pack(a_ref, u_ref)


def partners(row, rounds):
    found = []
    for low, high in rounds:
        for d in range(1, 1 << (high - low)):
            block = 1 << low
            digit = row // block % (1 << (high - low))
            flipped = 0
            for bit in range(high - low):
                own = digit // (1 << bit) % 2
                flipped = flipped + ((1 - own) if d >> bit & 1 else own) * (1 << bit)
            found.append(row + (flipped - digit) * block)
    return found


def exchange_kernel(u_ref, root_ref, col_ref, path_ref, tables_ref, grams_ref,
                    et_ref, out_buf, in_buf, send_sem, recv_sem, tab_send, tab_recv):
    row = lax.axis_index("row")
    col = lax.axis_index("col")
    rows = lax.axis_size("row")
    after = lax.rem(row + 1, rows)
    before = lax.rem(row + rows - 1, rows)
    others = partners(row, ROUNDS)
    mate = (row, 1 - col)

    barrier = pltpu.get_barrier_semaphore()
    for device in [mate, (before, col), (after, col)] + [(r, col) for r in others]:
        pl.semaphore_signal(barrier, inc=1, device_id=device, device_id_type=MESH)

    et_ref[8] = tripled(col_ref[col])
    for k in range(8):
        et_ref[k] = tripled(path_ref[k])
    part = folded(sandwich(et_ref[8], root_ref[...]))
    out_buf[0] = part
    pl.semaphore_wait(barrier, 3 + len(others))

    def send(slot, target, place):
        copy = pltpu.make_async_remote_copy(
            src_ref=out_buf.at[slot], dst_ref=in_buf.at[place],
            send_sem=send_sem.at[place], recv_sem=recv_sem.at[place],
            device_id=target, device_id_type=MESH)
        copy.start()
        return copy

    def table(source, place, sem, target):
        copy = pltpu.make_async_remote_copy(
            src_ref=source, dst_ref=tables_ref.at[place],
            send_sem=tab_send.at[sem], recv_sem=tab_recv.at[sem],
            device_id=target, device_id_type=MESH)
        copy.start()
        return copy

    chain = [send(0, mate, 0)]
    to_after = table(u_ref, 0 + col, 0, (after, col))
    to_before = table(u_ref, 4 + col, 1, (before, col))
    to_mate = table(u_ref, 2 + col, 2, mate)
    tables_ref[2 + col] = u_ref[...]

    chain[0].wait_recv()
    total = part + in_buf[0]
    grams = [unfolded(total)]
    place = 1
    slot = 1
    for low, high in ROUNDS:
        own = grams[-1]
        parts = []
        first = place
        for t in range(1, high - low + 1):
            own = sandwich(et_ref[low + t - 1], own)
            parts.append(folded(own))
            out_buf[slot] = parts[-1]
            for d in range(1 << (t - 1), 1 << t):
                chain.append(send(slot, (others[place - 1], col), place))
                place += 1
            slot += 1
        place = first
        for t in range(1, high - low + 1):
            if t == 1:
                total = parts[0]
            else:
                total = folded(sandwich(et_ref[low + t - 1], grams[-1]))
            for d in range(1 << (t - 1), 1 << t):
                chain[place].wait_recv()
                total = total + in_buf[place]
                place += 1
            grams.append(unfolded(total))
    unit = jnp.where(lax.broadcasted_iota(jnp.int32, (64, 64), 0)
                     == lax.broadcasted_iota(jnp.int32, (64, 64), 1), 1.0, 0.0)
    for b in range(8):
        grams_ref[:, b, :] = jnp.concatenate([grams[b], grams[8] if b == 0 else unit], axis=1)

    to_after.wait_recv()
    from_before = table(tables_ref.at[0 + col], 0 + col, 3, mate)
    to_before.wait_recv()
    from_after = table(tables_ref.at[4 + col], 4 + col, 4, mate)
    for copy in (to_mate, from_before, from_after):
        copy.wait_recv()
    for copy in (to_after, to_before, to_mate, from_before, from_after):
        copy.wait_send()
    for copy in chain:
        copy.wait_send()


def project_kernel(rows_ref, cols_ref, ct_ref, valid_ref, tables_ref, own_ref, grams_ref, out_ref, path_ref,
                   t_ref, o_ref, left_ref, right_ref, u_ref):
    chol_pack(grams_ref, u_ref)
    for k in range(9):
        path_ref[0, k] = u_ref[:, k % 8, (k // 8) * 64:(k // 8) * 64 + 64]

    def unpack(t, carry):
        for b in range(8):
            both = tables_ref[t, :, b, :]
            for half in range(2):
                h, l = split2(both[:, half * 64:half * 64 + 64])
                right_ref[t * ENTRIES + half * 8 + b] = jnp.concatenate([h, l], axis=1)
        return carry

    lax.fori_loop(0, 6, unpack, 0)
    for b in range(8):
        both = own_ref[:, b, :]
        for half in range(2):
            h, l = split2(both[:, half * 64:half * 64 + 64])
            left_ref[half * 8 + b] = jnp.concatenate([h, l, h], axis=1)

    def spread(p, carry):
        x = jnp.concatenate([ct_ref[p].astype(F32), ct_ref[p + 32].astype(F32)], axis=0)
        t_ref[p] = x.T
        return carry

    lax.fori_loop(0, 32, spread, 0, unroll=2)

    for first, slots, log_n, offset in LEVELS:
        unroll = min(slots, 64)

        def group(g, carry):
            for k in range(unroll):
                s = first + g * unroll + k
                r = rows_ref[s] + offset
                v = cols_ref[s]
                q = (v >> log_n) * ENTRIES + offset + (v & ((1 << log_n) - 1))
                c = t_ref[:, s, :].astype(BF)
                top = jnp.concatenate([c[:, :64], c[:, :64]], axis=1)
                low = jnp.concatenate([c[:, 64:], c[:, 64:]], axis=1)
                y = lax.dot_general(right_ref[q], jnp.concatenate([top, low], axis=0), NT,
                                    preferred_element_type=F32)
                h, l = split2(y)
                o = lax.dot_general(left_ref[r], jnp.concatenate([h, h, l], axis=1), NT,
                                    preferred_element_type=F32)
                o_ref[:, s, :] = folded(o)
            return carry

        lax.fori_loop(0, slots // unroll, group, 0)

    real = valid_ref[...] == 1

    def gather(p, carry):
        x = jnp.where(real, o_ref[p].T, 0.0).astype(BF)
        out_ref[p] = x[:64]
        out_ref[p + 32] = x[64:]
        return carry

    lax.fori_loop(0, 32, gather, 0, unroll=2)


def shards(leaf_basis, local_transfer, col_transfer, row_transfer, coupling, slot_block_row, block_col, block_valid):
    pack = jax.ShapeDtypeStruct((64, 8, 128), F32)
    limit = pltpu.CompilerParams(vmem_limit_bytes=56 * 2**20)
    factors, root = pl.pallas_call(
        local_kernel,
        out_shape=(pack, jax.ShapeDtypeStruct((64, 64), F32)),
        in_specs=[VMEM] * 2,
        out_specs=(VMEM, VMEM),
        scratch_shapes=[pltpu.VMEM((64, 8, 128), F32), pltpu.VMEM((14, 64, 192), BF)],
        compiler_params=limit,
        name="local_factors",
    )(leaf_basis.transpose(0, 2, 1), local_transfer)
    slots = 1 + sum((1 << (high - low)) - 1 for low, high in ROUNDS)
    tables, grams = pl.pallas_call(
        exchange_kernel,
        out_shape=(jax.ShapeDtypeStruct((6, 64, 8, 128), F32), pack),
        in_specs=[VMEM] * 4,
        out_specs=(VMEM, VMEM),
        scratch_shapes=[
            pltpu.VMEM((9, 64, 192), BF),
            pltpu.VMEM((9, 32, 128), F32),
            pltpu.VMEM((slots, 32, 128), F32),
            pltpu.SemaphoreType.DMA((slots,)),
            pltpu.SemaphoreType.DMA((slots,)),
            pltpu.SemaphoreType.DMA((5,)),
            pltpu.SemaphoreType.DMA((5,)),
        ],
        compiler_params=pltpu.CompilerParams(
            vmem_limit_bytes=56 * 2**20, collective_id=0, has_side_effects=True),
        name="exchange",
    )(factors, root, col_transfer[0], row_transfer[0])
    projected, path_factor = pl.pallas_call(
        project_kernel,
        out_shape=(jax.ShapeDtypeStruct((64, 64, 240), BF), jax.ShapeDtypeStruct((1, 9, 64, 64), F32)),
        in_specs=[SMEM, SMEM] + [VMEM] * 5,
        out_specs=(VMEM, VMEM),
        scratch_shapes=[
            pltpu.VMEM((32, 240, 128), F32),
            pltpu.VMEM((32, 240, 128), F32),
            pltpu.VMEM((ENTRIES, 64, 192), BF),
            pltpu.VMEM((6 * ENTRIES, 64, 128), BF),
            pltpu.VMEM((64, 8, 128), F32),
        ],
        compiler_params=limit,
        name="project",
    )(slot_block_row, block_col, coupling.transpose(1, 2, 0), block_valid[None], tables, factors, grams)
    return projected.transpose(2, 0, 1), path_factor


def solution(mesh):
    placed = (
        P(("row", "col"), None, None),
        P(("row", "col"), None, None),
        P("row", None, None, None),
        P("row", None, None, None),
        P(("row", "col"), None, None),
        P(("row", "col")),
        P(("row", "col")),
        P(("row", "col")),
    )
    return jax.shard_map(
        shards,
        mesh=mesh,
        in_specs=placed,
        out_specs=(P(("row", "col"), None, None), P(("row", "col"), None, None, None)),
        check_vma=False,
    )
```

time: 370 us -> 79.6 us (0.22)
  the two profiles are of different devices: /device:TPU:6 before, /device:TPU:1 now
where the time goes in v1:
time: 79.6 us; the launch traced here: 79.4 us
  Pallas kernels  78.8 us (99%)
    pallas_call x1, Pallas kernels, shards(): pl.pallas_call(exchange_kernel, out_shape=(jax.ShapeDtypeStruct((6, 64, 8...  41.9 us
    pallas_call x1, Pallas kernels, shards(): pl.pallas_call(project_kernel, out_shape=(jax.ShapeDtypeStruct((64, 64, 2...  26.7 us
    pallas_call x1, Pallas kernels, shards(): pl.pallas_call(local_kernel, out_shape=(pack, jax.ShapeDtypeStruct((64, 6...  10.2 us

profile of v1, /device:TPU:1, one launch (start us, length us, event | category | flops | bytes accessed | tf_op | source)
XLA Modules:
  0.0 79.4 jit_solution(8921511019607010853)
XLA Ops:
  0.6 10.2 %local_factors.1 = (f32[64,8,128]{2,1,0:T(8,128)}, f32[64,64]{1,0:T(8,128)}) custom-call(f32[8,64,128]{2,1,0:T(8,128)} %bitcast.7, bf16[14,64,64]{2,1,0:T(8,128)(2,1)} %transfer_ref.1), custom_call_target="tpu_custom_call" | custom-call | tf_op jit(solution)/shard_map/local_factors/pallas_call | solution.py:274
  10.8 41.9 %exchange.1 = (f32[6,64,8,128]{3,2,1,0:T(8,128)}, f32[64,8,128]{2,1,0:T(8,128)}) custom-call(f32[64,8,128]{2,1,0:T(8,128)} %get-tuple-element.8.u_ref.own_ref, f32[64,64]{1,0:T(8,128)} %get-tuple-element.9.root_ref, bf16[2,64,64]{2,1,0:T(8,128)(2,1)} %bitcast.9, bf16[8,64,64]{2,1,0:T(8,128)(2,1)} %bitcast.8), custom_call_target="tpu_custom_call" | custom-call | tf_op jit(solution)/shard_map/exchange/pallas_call | solution.py:284
  52.7 26.7 %project.1 = (bf16[64,64,240]{2,1,0:T(8,128)(2,1)}, f32[1,9,64,64]{3,2,1,0:T(8,128)}) custom-call(s32[240]{0:T(256)} %rows_ref.1, s32[240]{0:T(256)} %cols_ref.1, bf16[64,64,240]{2,1,0:T(8,128)(2,1)} %bitcast.6, s32[1,240]{1,0:T(1,128)} %bitcast.10, f32[6,64,8,128]{3,2,1,0:T(8,128)} %get-tuple-element.10.tables_ref, ...), custom_call_target="tpu_custom_call" | custom-call | tf_op jit(solution)/shard_map/project/pallas_call | solution.py:302

commit v2 on v1

v2 whole, which is shorter than its diff:
```python
import functools

import jax
import jax.numpy as jnp
from jax import lax
from jax.experimental import pallas as pl
from jax.experimental.pallas import tpu as pltpu
from jax.sharding import PartitionSpec as P

BF = jnp.bfloat16
F32 = jnp.float32
NT = (((1,), (1,)), ((), ()))
MESH = pl.DeviceIdType.MESH
VMEM = pl.BlockSpec(memory_space=pltpu.VMEM)
SMEM = pl.BlockSpec(memory_space=pltpu.SMEM)

PAIRS = ((0, 64, 2, 8), (64, 32, 1, 12), (96, 16, 0, 14), (112, 16, None, 0))
ROUNDS = ((0, 2), (2, 5), (5, 8))
COL = 14
PATH = 15
GROUP = 16
PACKED = 33


def split2(x):
    high = x.astype(BF)
    return high, (x - high.astype(F32)).astype(BF)


def split3(x):
    high = x.astype(BF)
    rest = x - high.astype(F32)
    middle = rest.astype(BF)
    return high, middle, (rest - middle.astype(F32)).astype(BF)


def dot_nt(a, b):
    return lax.dot_general(a, b, NT, preferred_element_type=F32)


def gram(xt):
    h, m, l = split3(xt)
    left = jnp.concatenate([h, h, m, h, l, m], axis=1)
    right = jnp.concatenate([h, m, h, l, h, m], axis=1)
    return lax.dot_general(left, right, NT, preferred_element_type=F32)


def tripled(transfer):
    et = transfer.astype(F32).T.astype(BF)
    return jnp.concatenate([et, et, et], axis=1)


def sandwich(et3, g):
    y = lax.dot_general(et3, jnp.concatenate(split3(g), axis=1), NT, preferred_element_type=F32)
    return lax.dot_general(jnp.concatenate(split3(y), axis=1), et3, NT, preferred_element_type=F32)


def folded(g):
    return jnp.concatenate([g[:32], g[32:]], axis=1)


def unfolded(g):
    return jnp.concatenate([g[:, :64], g[:, 64:]], axis=0)


def take(row, index):
    return jnp.take_along_axis(row, index, axis=1, mode="promise_in_bounds")


def factor_blocks(a_ref, u_ref, low, high):
    lane = lax.broadcasted_iota(jnp.int32, (8, 128), 1)
    half = lane // 64 * 64
    column = lane % 64

    def block(number, carry):
        first = number * 8
        index = [half + (first + i) for i in range(8)]

        def update(g, rows):
            done = [u_ref[g * 8 + m] for m in range(8)]
            fresh = []
            for i in range(8):
                terms = [take(done[m], index[i]) * done[m] for m in range(8)]
                while len(terms) > 1:
                    terms = [terms[k] + terms[k + 1] for k in range(0, len(terms), 2)]
                fresh.append(rows[i] - terms[0])
            return tuple(fresh)

        rows = list(lax.fori_loop(0, number, update, tuple(a_ref[first + i] for i in range(8))))
        entry = {}
        for j in range(8):
            for i in range(j + 1):
                entry[i, j] = take(rows[i], index[j])
        for k in range(8):
            scale = lax.rsqrt(entry[k, k])
            top = rows[k] * scale
            u_ref[first + k] = jnp.where(column < first + k, 0.0, top)
            factor = {j: entry[k, j] * scale for j in range(k + 1, 8)}
            for i in range(k + 1, 8):
                rows[i] = rows[i] - factor[i] * top
                for j in range(i, 8):
                    entry[i, j] = entry[i, j] - factor[i] * factor[j]
        return carry

    lax.fori_loop(low, high, block, 0)


def partners(row, rounds):
    found = []
    for low, high in rounds:
        for d in range(1, 1 << (high - low)):
            block = 1 << low
            digit = row // block % (1 << (high - low))
            flipped = 0
            for bit in range(high - low):
                own = digit // (1 << bit) % 2
                flipped = flipped + ((1 - own) if d >> bit & 1 else own) * (1 << bit)
            found.append(row + (flipped - digit) * block)
    return found


def local_grams(leaf_ref, et_ref):
    level = [gram(leaf_ref[i]) for i in range(8)]
    grams = list(level)
    offset = 0
    while len(level) > 1:
        parts = [sandwich(et_ref[offset + i], g) for i, g in enumerate(level)]
        offset += len(level)
        level = [parts[i] + parts[i + 1] for i in range(0, len(parts), 2)]
        grams += level
    return grams


def pack_triangles(u_ref, packed_ref):
    column = lax.broadcasted_iota(jnp.int32, (8, 128), 1) % 64
    packed_ref[0] = u_ref[0]
    packed_ref[32] = u_ref[32]
    for i in range(1, 32):
        packed_ref[i] = jnp.where(column >= i, u_ref[i], pltpu.roll(u_ref[64 - i], i, 1))


def unpack_triangles(packed_ref, u_ref):
    column = lax.broadcasted_iota(jnp.int32, (8, 128), 1) % 64
    u_ref[0] = packed_ref[0]
    u_ref[32] = packed_ref[32]
    for i in range(1, 32):
        both = packed_ref[i]
        u_ref[i] = jnp.where(column >= i, both, 0.0)
        u_ref[64 - i] = pltpu.roll(jnp.where(column >= i, 0.0, both), 128 - i, 1)


def main_kernel(rows_ref, cols_ref, leaf_ref, local_ref, col_ref, path_ref, ct_hbm, valid_ref, out_hbm, grams_ref,
                et_ref, a_ref, u_ref, g_ref, ct_ref, t_ref, o_ref, out_ref, table_ref, full_ref, left_ref, low_ref,
                high_ref, out_buf, in_buf, send_sem, recv_sem, tab_send, tab_recv, local_sem):
    row = lax.axis_index("row")
    col = lax.axis_index("col")
    rows = lax.axis_size("row")
    after = lax.rem(row + 1, rows)
    before = lax.rem(row + rows - 1, rows)
    others = partners(row, ROUNDS)
    mate = (row, 1 - col)
    left = lax.broadcasted_iota(jnp.int32, (64, 128), 1) < 64

    fetch = pltpu.make_async_copy(ct_hbm, ct_ref, local_sem.at[0])
    fetch.start()
    barrier = pltpu.get_barrier_semaphore()
    for device in [mate, (before, col), (after, col)] + [(r, col) for r in others]:
        pl.semaphore_signal(barrier, inc=1, device_id=device, device_id_type=MESH)

    def send(slot, target, place):
        copy = pltpu.make_async_remote_copy(
            src_ref=out_buf.at[slot], dst_ref=in_buf.at[place],
            send_sem=send_sem.at[place], recv_sem=recv_sem.at[place],
            device_id=target, device_id_type=MESH)
        copy.start()
        return copy

    def send_table(place, sem, target, there):
        copy = pltpu.make_async_remote_copy(
            src_ref=table_ref.at[place], dst_ref=table_ref.at[there],
            send_sem=tab_send.at[sem], recv_sem=tab_recv.at[sem],
            device_id=target, device_id_type=MESH)
        copy.start()
        return copy

    chain = []
    starts = []
    for low, high in ROUNDS:
        starts.append((1 + sum((1 << (b - a)) - 1 for a, b in ROUNDS if a < low), low, high))

    def send_round(number):
        first, low, high = starts[number]
        own = g_ref[low]
        place = first
        for t in range(1, high - low + 1):
            own = sandwich(et_ref[PATH + low + t - 1], own)
            out_buf[low + t] = folded(own)
            for d in range(1 << (t - 1), 1 << t):
                chain.append(send(low + t, (others[place - 1], col), place))
                place += 1

    def end_round(number):
        first, low, high = starts[number]
        place = first
        for t in range(1, high - low + 1):
            if t == 1:
                total = out_buf[low + 1]
            else:
                total = folded(sandwich(et_ref[PATH + low + t - 1], g_ref[low + t - 1]))
            for d in range(1 << (t - 1), 1 << t):
                chain[place].wait_recv()
                total = total + in_buf[place]
                place += 1
            g_ref[low + t] = unfolded(total)

    for i in range(14):
        et_ref[i] = tripled(local_ref[i])
    et_ref[COL] = tripled(col_ref[col])
    grams = local_grams(leaf_ref, et_ref)
    out_buf[0] = folded(sandwich(et_ref[COL], grams[14]))
    pl.semaphore_wait(barrier, 3 + len(others))
    chain.append(send(0, mate, 0))

    unit = jnp.where(lax.broadcasted_iota(jnp.int32, (64, 64), 0)
                     == lax.broadcasted_iota(jnp.int32, (64, 64), 1), 1.0, 0.0)
    grams.append(unit)
    for b in range(8):
        a_ref[:, b, :] = jnp.concatenate([grams[b], grams[8 + b]], axis=1)
    for k in range(8):
        et_ref[PATH + k] = tripled(path_ref[k])
    chain[0].wait_recv()
    g_ref[0] = unfolded(out_buf[0] + in_buf[0])
    send_round(0)
    factor_blocks(a_ref, u_ref, 0, 5)
    end_round(0)
    send_round(1)
    factor_blocks(a_ref, u_ref, 5, 8)
    mine = 2 + col
    pack_triangles(u_ref, table_ref.at[mine])
    to_after = send_table(mine, 0, (after, col), col)
    to_before = send_table(mine, 1, (before, col), 4 + col)
    to_mate = send_table(mine, 2, mate, mine)
    end_round(1)
    send_round(2)

    fetch.wait()
    pad = jnp.zeros((64, 16), F32)

    def spread(j, carry):
        x = ct_ref[j].astype(F32)
        later = jnp.concatenate([x[:, 128:], pad], axis=1)
        t_ref[j] = jnp.concatenate([x[:, :128], later], axis=0).T
        return carry

    lax.fori_loop(0, 64, spread, 0, unroll=4)

    for b in range(8):
        both = u_ref[:, b, :]
        for half in range(2):
            x = jnp.concatenate(split2(both[:, half * 64:half * 64 + 64]), axis=1)
            left_ref[half * 8 + b] = jnp.concatenate([x, x], axis=1)

    to_after.wait_recv()
    from_before = send_table(col, 3, mate, col)
    to_before.wait_recv()
    from_after = send_table(4 + col, 4, mate, 4 + col)
    to_mate.wait_recv()
    from_before.wait_recv()
    from_after.wait_recv()

    def unpack(t, carry):
        unpack_triangles(table_ref.at[t], full_ref)
        for b in range(8):
            h, l = split2(full_ref[:, b, :])
            zero = jnp.zeros_like(h)
            low_ref[t * 8 + b] = jnp.concatenate([jnp.where(left, h, zero), jnp.where(left, l, zero)], axis=1)
            high_ref[t * 8 + b] = jnp.concatenate([jnp.where(left, zero, h), jnp.where(left, zero, l)], axis=1)
        return carry

    lax.fori_loop(0, 6, unpack, 0)

    for start, count, log_n, offset in PAIRS:
        def group(g, carry):
            for k in range(GROUP):
                p = start + g * GROUP + k
                v = cols_ref[p]
                right_a = low_ref[v]
                left_a = left_ref[rows_ref[p]]
                if log_n is None:
                    right_b = high_ref[0]
                    left_b = left_ref[0]
                else:
                    v = cols_ref[p + 128]
                    right_b = high_ref[(v >> log_n) * 8 + (offset - 8) + (v & ((1 << log_n) - 1))]
                    left_b = left_ref[rows_ref[p + 128] + offset]
                c = t_ref[:, p, :].astype(BF)
                c = jnp.concatenate([c, c], axis=1)
                y = dot_nt(jnp.concatenate([right_a, right_b], axis=0), jnp.concatenate([c, c], axis=0))
                o = dot_nt(jnp.concatenate([left_a, left_b], axis=0), jnp.concatenate(split2(y), axis=1))
                o_ref[:, p, :] = jnp.where(left, o[:64], o[64:])
            return carry

        lax.fori_loop(0, count // GROUP, group, 0)

    real = valid_ref[...] == 1

    def gather(i, carry):
        x = o_ref[i].T
        x = jnp.concatenate([x[:64], x[64:, :112]], axis=1)
        out_ref[i] = jnp.where(real, x, 0.0).astype(BF)
        return carry

    lax.fori_loop(0, 64, gather, 0, unroll=4)
    store = pltpu.make_async_copy(out_ref, out_hbm, local_sem.at[1])
    store.start()

    end_round(2)
    for b in range(8):
        grams_ref[:, b, :] = jnp.concatenate([g_ref[b], g_ref[8] if b == 0 else unit], axis=1)
    store.wait()
    for copy in (to_after, to_before, to_mate, from_before, from_after):
        copy.wait_send()
    for copy in chain:
        copy.wait_send()


def path_kernel(blocks_hbm, grams_ref, out_hbm, path_ref, u_ref, sem):
    copy = pltpu.make_async_copy(blocks_hbm, out_hbm, sem)
    copy.start()
    factor_blocks(grams_ref, u_ref, 0, 8)
    for k in range(9):
        path_ref[0, k] = u_ref[:, k % 8, (k // 8) * 64:(k // 8) * 64 + 64]
    copy.wait()


def shards(leaf_basis, local_transfer, col_transfer, row_transfer, coupling, slot_block_row, block_col, block_valid):
    blocks = jax.ShapeDtypeStruct((64, 64, 240), BF)
    places = 1 + sum((1 << (high - low)) - 1 for low, high in ROUNDS)
    hbm = pl.BlockSpec(memory_space=pl.ANY)
    projected, grams = pl.pallas_call(
        main_kernel,
        out_shape=(blocks, jax.ShapeDtypeStruct((64, 8, 128), F32)),
        in_specs=[SMEM, SMEM, VMEM, VMEM, VMEM, VMEM, hbm, VMEM],
        out_specs=(hbm, VMEM),
        scratch_shapes=[
            pltpu.VMEM((23, 64, 192), BF),
            pltpu.VMEM((64, 8, 128), F32),
            pltpu.VMEM((64, 8, 128), F32),
            pltpu.VMEM((9, 64, 64), F32),
            pltpu.VMEM((64, 64, 240), BF),
            pltpu.VMEM((64, 128, 128), F32),
            pltpu.VMEM((64, 128, 128), F32),
            pltpu.VMEM((64, 64, 240), BF),
            pltpu.VMEM((6, PACKED, 8, 128), F32),
            pltpu.VMEM((64, 8, 128), F32),
            pltpu.VMEM((16, 64, 256), BF),
            pltpu.VMEM((48, 64, 256), BF),
            pltpu.VMEM((48, 64, 256), BF),
            pltpu.VMEM((9, 32, 128), F32),
            pltpu.VMEM((places, 32, 128), F32),
            pltpu.SemaphoreType.DMA((places,)),
            pltpu.SemaphoreType.DMA((places,)),
            pltpu.SemaphoreType.DMA((5,)),
            pltpu.SemaphoreType.DMA((5,)),
            pltpu.SemaphoreType.DMA((2,)),
        ],
        compiler_params=pltpu.CompilerParams(
            vmem_limit_bytes=60 * 2**20, collective_id=0, has_side_effects=True),
        name="upsweep_and_projection",
    )(slot_block_row, block_col, leaf_basis.transpose(0, 2, 1), local_transfer, col_transfer[0], row_transfer[0],
      coupling.transpose(1, 2, 0), block_valid[None])
    projected, path_factor = pl.pallas_call(
        path_kernel,
        out_shape=(blocks, jax.ShapeDtypeStruct((1, 9, 64, 64), F32)),
        in_specs=[hbm, VMEM],
        out_specs=(hbm, VMEM),
        scratch_shapes=[pltpu.VMEM((64, 8, 128), F32), pltpu.SemaphoreType.DMA(())],
        compiler_params=pltpu.CompilerParams(vmem_limit_bytes=60 * 2**20),
        name="path_factors",
    )(projected, grams)
    return projected.transpose(2, 0, 1), path_factor


def solution(mesh):
    placed = (
        P(("row", "col"), None, None),
        P(("row", "col"), None, None),
        P("row", None, None, None),
        P("row", None, None, None),
        P(("row", "col"), None, None),
        P(("row", "col")),
        P(("row", "col")),
        P(("row", "col")),
    )
    return jax.shard_map(
        shards,
        mesh=mesh,
        in_specs=placed,
        out_specs=(P(("row", "col"), None, None), P(("row", "col"), None, None, None)),
        check_vma=False,
    )
```

time: 79.6 us -> 122 us (1.53)
  Pallas kernels: 78.8 us -> 122 us
    pallas_call x3 -> x2, Pallas kernels: 78.8 us -> 122 us  [the longest x1 66.3 us: shards(): pl.pallas_call(path_kernel, out_shape=(blocks, jax.ShapeDtypeStruct((1, 9...]
where the time goes in v2:
time: 122 us
  Pallas kernels  122 us (100%)
    pallas_call x1, Pallas kernels, shards(): pl.pallas_call(path_kernel, out_shape=(blocks, jax.ShapeDtypeStruct((1, 9...  66.3 us
    pallas_call x1, Pallas kernels, shards(): pl.pallas_call(main_kernel, out_shape=(blocks, jax.ShapeDtypeStruct((64,...  55.3 us

profile of v2, /device:TPU:1, one launch (start us, length us, event | category | flops | bytes accessed | tf_op | source)
XLA Modules:
  0.0 122.2 jit_solution(12263305530848856758)
XLA Ops:
  0.6 55.3 %upsweep_and_projection.1 = (bf16[64,64,240]{2,1,0:T(8,128)(2,1)}, f32[64,8,128]{2,1,0:T(8,128)}) custom-call(s32[240]{0:T(256)} %rows_ref.1, s32[240]{0:T(256)} %cols_ref.1, f32[8,64,128]{2,1,0:T(8,128)} %bitcast.7, bf16[14,64,64]{2,1,0:T(8,128)(2,1)} %local_ref.1, bf16[2,64,64]{2,1,0:T(8,128)(2,1)} %bitcast.9, bf16[8,64,64]{2,1,0:T(8,128)(2,1)} %bitcast.8, ...), custom_call_target="tpu_custom_call" | custom-call | tf_op jit(solution)/shard_map/upsweep_and_projection/pallas_call | solution.py:340
  55.9 66.3 %path_factors.1 = (bf16[64,64,240]{2,1,0:T(8,128)(2,1)}, f32[1,9,64,64]{3,2,1,0:T(8,128)}) custom-call(bf16[64,64,240]{2,1,0:T(8,128)(2,1)} %get-tuple-element.6.blocks_hbm, f32[64,8,128]{2,1,0:T(8,128)} %get-tuple-element.7.grams_ref), custom_call_target="tpu_custom_call" | custom-call | tf_op jit(solution)/shard_map/path_factors/pallas_call | solution.py:372

commit v3 on v2

--- a/solution.py
+++ b/solution.py
@@ -14,11 +14,11 @@
 VMEM = pl.BlockSpec(memory_space=pltpu.VMEM)
 SMEM = pl.BlockSpec(memory_space=pltpu.SMEM)
 
-PAIRS = ((0, 64, 2, 8), (64, 32, 1, 12), (96, 16, 0, 14), (112, 16, None, 0))
+PAIRS = ((0, 64, 2, 8), (64, 32, 1, 12), (96, 16, 0, 14), (112, 16, None, None))
 ROUNDS = ((0, 2), (2, 5), (5, 8))
 COL = 14
 PATH = 15
-GROUP = 16
+GROUP = 32
 PACKED = 33
 
 
@@ -150,7 +150,7 @@
 
 
 def main_kernel(rows_ref, cols_ref, leaf_ref, local_ref, col_ref, path_ref, ct_hbm, valid_ref, out_hbm, grams_ref,
-                et_ref, a_ref, u_ref, g_ref, ct_ref, t_ref, o_ref, out_ref, table_ref, full_ref, left_ref, low_ref,
+                et_ref, a_ref, u_ref, g_ref, ct_ref, t_ref, o_ref, y_ref, out_ref, table_ref, full_ref, left_ref, low_ref,
                 high_ref, out_buf, in_buf, send_sem, recv_sem, tab_send, tab_recv, local_sem):
     row = lax.axis_index("row")
     col = lax.axis_index("col")
@@ -213,6 +213,12 @@
                 place += 1
             g_ref[low + t] = unfolded(total)
 
+    def store_table(t):
+        for b in range(8):
+            x = full_ref[:, b, :]
+            low_ref[t * 8 + b] = jnp.concatenate(split2(jnp.where(left, x, 0.0)), axis=1)
+            high_ref[t * 8 + b] = jnp.concatenate(split2(jnp.where(left, 0.0, x)), axis=1)
+
     for i in range(14):
         et_ref[i] = tripled(local_ref[i])
     et_ref[COL] = tripled(col_ref[col])
@@ -228,37 +234,74 @@
         a_ref[:, b, :] = jnp.concatenate([grams[b], grams[8 + b]], axis=1)
     for k in range(8):
         et_ref[PATH + k] = tripled(path_ref[k])
+
+    fetch.wait()
+    pad = jnp.zeros((64, 16), F32)
+
+    def spread(j, carry):
+        x = ct_ref[j].astype(F32)
+        later = jnp.concatenate([x[:, 128:], pad], axis=1)
+        t_ref[:, j, :] = jnp.concatenate([x[:, :128], later], axis=0).T
+        return carry
+
+    lax.fori_loop(0, 64, spread, 0, unroll=4)
+
     chain[0].wait_recv()
     g_ref[0] = unfolded(out_buf[0] + in_buf[0])
     send_round(0)
-    factor_blocks(a_ref, u_ref, 0, 5)
-    end_round(0)
-    send_round(1)
-    factor_blocks(a_ref, u_ref, 5, 8)
+
+    factor_blocks(a_ref, u_ref, 0, 8)
     mine = 2 + col
     pack_triangles(u_ref, table_ref.at[mine])
     to_after = send_table(mine, 0, (after, col), col)
     to_before = send_table(mine, 1, (before, col), 4 + col)
     to_mate = send_table(mine, 2, mate, mine)
-    end_round(1)
-    send_round(2)
-
-    fetch.wait()
-    pad = jnp.zeros((64, 16), F32)
-
-    def spread(j, carry):
-        x = ct_ref[j].astype(F32)
-        later = jnp.concatenate([x[:, 128:], pad], axis=1)
-        t_ref[j] = jnp.concatenate([x[:, :128], later], axis=0).T
-        return carry
-
-    lax.fori_loop(0, 64, spread, 0, unroll=4)
+    end_round(0)
+    send_round(1)
 
     for b in range(8):
         both = u_ref[:, b, :]
         for half in range(2):
-            x = jnp.concatenate(split2(both[:, half * 64:half * 64 + 64]), axis=1)
-            left_ref[half * 8 + b] = jnp.concatenate([x, x], axis=1)
+            left_ref[half * 8 + b] = jnp.concatenate(split2(both[:, half * 64:half * 64 + 64]), axis=1)
+
+    def row_products(start, count, offset):
+        def group(g, carry):
+            for k in range(min(GROUP, count)):
+                p = start + g * GROUP + k
+                first = left_ref[rows_ref[p]]
+                second = left_ref[0] if offset is None else left_ref[rows_ref[p + 128] + offset]
+                c = t_ref[p].astype(BF)
+                y = jnp.dot(jnp.concatenate([first, second], axis=0), jnp.concatenate([c, c], axis=0),
+                            preferred_element_type=F32)
+                h, l = split2(jnp.where(left, y[:64], y[64:]))
+                y_ref[p] = jnp.concatenate([h, l], axis=0)
+            return carry
+
+        lax.fori_loop(0, max(1, count // GROUP), group, 0)
+
+    def column_products(start, count, log_n, offset):
+        def group(g, carry):
+            for k in range(min(GROUP, count)):
+                p = start + g * GROUP + k
+                first = low_ref[cols_ref[p]]
+                if offset is None:
+                    second = high_ref[0]
+                else:
+                    v = cols_ref[p + 128]
+                    second = high_ref[(v >> log_n) * 8 + (offset - 8) + (v & ((1 << log_n) - 1))]
+                x = jnp.concatenate([first[:, :128], second[:, :128], first[:, 128:], second[:, 128:]], axis=0)
+                o = dot_nt(y_ref[p], x)
+                o = o[:64] + o[64:]
+                o_ref[p] = o[:, :128] + o[:, 128:]
+            return carry
+
+        lax.fori_loop(0, max(1, count // GROUP), group, 0)
+
+    for start, count, log_n, offset in PAIRS:
+        row_products(start, count, offset)
+
+    end_round(1)
+    send_round(2)
 
     to_after.wait_recv()
     from_before = send_table(col, 3, mate, col)
@@ -270,42 +313,18 @@
 
     def unpack(t, carry):
         unpack_triangles(table_ref.at[t], full_ref)
-        for b in range(8):
-            h, l = split2(full_ref[:, b, :])
-            zero = jnp.zeros_like(h)
-            low_ref[t * 8 + b] = jnp.concatenate([jnp.where(left, h, zero), jnp.where(left, l, zero)], axis=1)
-            high_ref[t * 8 + b] = jnp.concatenate([jnp.where(left, zero, h), jnp.where(left, zero, l)], axis=1)
+        store_table(t)
         return carry
 
     lax.fori_loop(0, 6, unpack, 0)
 
     for start, count, log_n, offset in PAIRS:
-        def group(g, carry):
-            for k in range(GROUP):
-                p = start + g * GROUP + k
-                v = cols_ref[p]
-                right_a = low_ref[v]
-                left_a = left_ref[rows_ref[p]]
-                if log_n is None:
-                    right_b = high_ref[0]
-                    left_b = left_ref[0]
-                else:
-                    v = cols_ref[p + 128]
-                    right_b = high_ref[(v >> log_n) * 8 + (offset - 8) + (v & ((1 << log_n) - 1))]
-                    left_b = left_ref[rows_ref[p + 128] + offset]
-                c = t_ref[:, p, :].astype(BF)
-                c = jnp.concatenate([c, c], axis=1)
-                y = dot_nt(jnp.concatenate([right_a, right_b], axis=0), jnp.concatenate([c, c], axis=0))
-                o = dot_nt(jnp.concatenate([left_a, left_b], axis=0), jnp.concatenate(split2(y), axis=1))
-                o_ref[:, p, :] = jnp.where(left, o[:64], o[64:])
-            return carry
-
-        lax.fori_loop(0, count // GROUP, group, 0)
+        column_products(start, count, log_n, offset)
 
     real = valid_ref[...] == 1
 
     def gather(i, carry):
-        x = o_ref[i].T
+        x = o_ref[:, i, :].T
         x = jnp.concatenate([x[:64], x[64:, :112]], axis=1)
         out_ref[i] = jnp.where(real, x, 0.0).astype(BF)
         return carry
@@ -324,13 +343,17 @@
         copy.wait_send()
 
 
-def path_kernel(blocks_hbm, grams_ref, out_hbm, path_ref, u_ref, sem):
-    copy = pltpu.make_async_copy(blocks_hbm, out_hbm, sem)
-    copy.start()
-    factor_blocks(grams_ref, u_ref, 0, 8)
+def path_kernel(blocks_hbm, grams_ref, out_hbm, path_ref, u_ref, blocks_ref, sem):
+    fetch = pltpu.make_async_copy(blocks_hbm, blocks_ref, sem.at[0])
+    store = pltpu.make_async_copy(blocks_ref, out_hbm, sem.at[1])
+    fetch.start()
+    factor_blocks(grams_ref, u_ref, 0, 4)
+    fetch.wait()
+    store.start()
+    factor_blocks(grams_ref, u_ref, 4, 8)
     for k in range(9):
         path_ref[0, k] = u_ref[:, k % 8, (k // 8) * 64:(k // 8) * 64 + 64]
-    copy.wait()
+    store.wait()
 
 
 def shards(leaf_basis, local_transfer, col_transfer, row_transfer, coupling, slot_block_row, block_col, block_valid):
@@ -348,12 +371,13 @@
             pltpu.VMEM((64, 8, 128), F32),
             pltpu.VMEM((9, 64, 64), F32),
             pltpu.VMEM((64, 64, 240), BF),
-            pltpu.VMEM((64, 128, 128), F32),
-            pltpu.VMEM((64, 128, 128), F32),
+            pltpu.VMEM((128, 64, 128), F32),
+            pltpu.VMEM((128, 64, 128), F32),
+            pltpu.VMEM((128, 128, 128), BF),
             pltpu.VMEM((64, 64, 240), BF),
             pltpu.VMEM((6, PACKED, 8, 128), F32),
             pltpu.VMEM((64, 8, 128), F32),
-            pltpu.VMEM((16, 64, 256), BF),
+            pltpu.VMEM((16, 64, 128), BF),
             pltpu.VMEM((48, 64, 256), BF),
             pltpu.VMEM((48, 64, 256), BF),
             pltpu.VMEM((9, 32, 128), F32),
@@ -374,7 +398,11 @@
         out_shape=(blocks, jax.ShapeDtypeStruct((1, 9, 64, 64), F32)),
         in_specs=[hbm, VMEM],
         out_specs=(hbm, VMEM),
-        scratch_shapes=[pltpu.VMEM((64, 8, 128), F32), pltpu.SemaphoreType.DMA(())],
+        scratch_shapes=[
+            pltpu.VMEM((64, 8, 128), F32),
+            pltpu.VMEM((64, 64, 240), BF),
+            pltpu.SemaphoreType.DMA((2,)),
+        ],
         compiler_params=pltpu.CompilerParams(vmem_limit_bytes=60 * 2**20),
         name="path_factors",
     )(projected, grams)

time: 122 us -> 55.7 us (0.46)
  Pallas kernels: 122 us -> 54.7 us
    pallas_call x1, Pallas kernels: 66.3 us -> 7.71 us  [shards(): pl.pallas_call(path_kernel, out_shape=(blocks, jax.ShapeDtypeStruct((1, 9...]
    pallas_call x1, Pallas kernels: 55.3 us -> 47 us  [shards(): pl.pallas_call(main_kernel, out_shape=(blocks, jax.ShapeDtypeStruct((64,...]
where the time goes in v3:
time: 55.7 us; the launch traced here: 55.3 us
  Pallas kernels  54.7 us (98%)
  between operations  0.64 us (1%)
    pallas_call x1, Pallas kernels, shards(): pl.pallas_call(main_kernel, out_shape=(blocks, jax.ShapeDtypeStruct((64,...  47 us
    pallas_call x1, Pallas kernels, shards(): pl.pallas_call(path_kernel, out_shape=(blocks, jax.ShapeDtypeStruct((1, 9...  7.71 us

profile of v3, /device:TPU:1, one launch (start us, length us, event | category | flops | bytes accessed | tf_op | source)
XLA Modules:
  0.0 55.3 jit_solution(14524379075715542838)
XLA Ops:
  0.6 47.0 %upsweep_and_projection.1 = (bf16[64,64,240]{2,1,0:T(8,128)(2,1)}, f32[64,8,128]{2,1,0:T(8,128)}) custom-call(s32[240]{0:T(256)} %rows_ref.1, s32[240]{0:T(256)} %cols_ref.1, f32[8,64,128]{2,1,0:T(8,128)} %bitcast.7, bf16[14,64,64]{2,1,0:T(8,128)(2,1)} %local_ref.1, bf16[2,64,64]{2,1,0:T(8,128)(2,1)} %bitcast.9, bf16[8,64,64]{2,1,0:T(8,128)(2,1)} %bitcast.8, ...), custom_call_target="tpu_custom_call" | custom-call | tf_op jit(solution)/shard_map/upsweep_and_projection/pallas_call | solution.py:363
  47.6 7.7 %path_factors.1 = (bf16[64,64,240]{2,1,0:T(8,128)(2,1)}, f32[1,9,64,64]{3,2,1,0:T(8,128)}) custom-call(bf16[64,64,240]{2,1,0:T(8,128)(2,1)} %get-tuple-element.6.blocks_hbm, f32[64,8,128]{2,1,0:T(8,128)} %get-tuple-element.7.grams_ref), custom_call_target="tpu_custom_call" | custom-call | tf_op jit(solution)/shard_map/path_factors/pallas_call | solution.py:396

commit v4 on v3

--- a/solution.py
+++ b/solution.py
@@ -67,12 +67,14 @@
     return jnp.take_along_axis(row, index, axis=1, mode="promise_in_bounds")
 
 
-def factor_blocks(a_ref, u_ref, low, high):
+def factor_blocks(a_ref, u_ref, low, high, beside=None, before=None, after=None):
     lane = lax.broadcasted_iota(jnp.int32, (8, 128), 1)
     half = lane // 64 * 64
     column = lane % 64
 
     def block(number, carry):
+        if before is not None:
+            before(number)
         first = number * 8
         index = [half + (first + i) for i in range(8)]
 
@@ -87,6 +89,8 @@
             return tuple(fresh)
 
         rows = list(lax.fori_loop(0, number, update, tuple(a_ref[first + i] for i in range(8))))
+        if beside is not None:
+            beside(number)
         entry = {}
         for j in range(8):
             for i in range(j + 1):
@@ -100,6 +104,8 @@
                 rows[i] = rows[i] - factor[i] * top
                 for j in range(i, 8):
                     entry[i, j] = entry[i, j] - factor[i] * factor[j]
+        if after is not None:
+            after(number)
         return carry
 
     lax.fori_loop(low, high, block, 0)
@@ -149,8 +155,8 @@
         u_ref[64 - i] = pltpu.roll(jnp.where(column >= i, 0.0, both), 128 - i, 1)
 
 
-def main_kernel(rows_ref, cols_ref, leaf_ref, local_ref, col_ref, path_ref, ct_hbm, valid_ref, out_hbm, grams_ref,
-                et_ref, a_ref, u_ref, g_ref, ct_ref, t_ref, o_ref, y_ref, out_ref, table_ref, full_ref, left_ref, low_ref,
+def main_kernel(rows_ref, cols_ref, leaf_ref, local_ref, col_ref, path_ref, ct_hbm, out_hbm, grams_ref,
+                et_ref, a_ref, u_ref, g_ref, ct_ref, t_ref, o_ref, y_ref, table_ref, full_ref, left_ref, low_ref,
                 high_ref, out_buf, in_buf, send_sem, recv_sem, tab_send, tab_recv, local_sem):
     row = lax.axis_index("row")
     col = lax.axis_index("col")
@@ -213,9 +219,9 @@
                 place += 1
             g_ref[low + t] = unfolded(total)
 
-    def store_table(t):
+    def store_table(t, source):
         for b in range(8):
-            x = full_ref[:, b, :]
+            x = source[:, b, :]
             low_ref[t * 8 + b] = jnp.concatenate(split2(jnp.where(left, x, 0.0)), axis=1)
             high_ref[t * 8 + b] = jnp.concatenate(split2(jnp.where(left, 0.0, x)), axis=1)
 
@@ -238,19 +244,17 @@
     fetch.wait()
     pad = jnp.zeros((64, 16), F32)
 
-    def spread(j, carry):
-        x = ct_ref[j].astype(F32)
-        later = jnp.concatenate([x[:, 128:], pad], axis=1)
-        t_ref[:, j, :] = jnp.concatenate([x[:, :128], later], axis=0).T
-        return carry
-
-    lax.fori_loop(0, 64, spread, 0, unroll=4)
-
+    def spread(number):
+        for k in range(8):
+            x = ct_ref[number * 8 + k].astype(F32)
+            later = jnp.concatenate([x[:, 128:], pad], axis=1)
+            t_ref[:, number * 8 + k, :] = jnp.concatenate([x[:, :128], later], axis=0).T
+
+    factor_blocks(a_ref, u_ref, 0, 3, spread)
     chain[0].wait_recv()
     g_ref[0] = unfolded(out_buf[0] + in_buf[0])
     send_round(0)
-
-    factor_blocks(a_ref, u_ref, 0, 8)
+    factor_blocks(a_ref, u_ref, 3, 8, spread)
     mine = 2 + col
     pack_triangles(u_ref, table_ref.at[mine])
     to_after = send_table(mine, 0, (after, col), col)
@@ -258,11 +262,6 @@
     to_mate = send_table(mine, 2, mate, mine)
     end_round(0)
     send_round(1)
-
-    for b in range(8):
-        both = u_ref[:, b, :]
-        for half in range(2):
-            left_ref[half * 8 + b] = jnp.concatenate(split2(both[:, half * 64:half * 64 + 64]), axis=1)
 
     def row_products(start, count, offset):
         def group(g, carry):
@@ -292,78 +291,100 @@
                 x = jnp.concatenate([first[:, :128], second[:, :128], first[:, 128:], second[:, 128:]], axis=0)
                 o = dot_nt(y_ref[p], x)
                 o = o[:64] + o[64:]
-                o_ref[p] = o[:, :128] + o[:, 128:]
+                o_ref[:, p, :] = o[:, :128] + o[:, 128:]
             return carry
 
         lax.fori_loop(0, max(1, count // GROUP), group, 0)
 
+    for b in range(8):
+        both = u_ref[:, b, :]
+        for half in range(2):
+            left_ref[half * 8 + b] = jnp.concatenate(split2(both[:, half * 64:half * 64 + 64]), axis=1)
+
+    store_table(mine, u_ref)
     for start, count, log_n, offset in PAIRS:
         row_products(start, count, offset)
 
     end_round(1)
     send_round(2)
 
+    def open_table(t):
+        unpack_triangles(table_ref.at[t], full_ref)
+        store_table(t, full_ref)
+
+    to_mate.wait_recv()
+    open_table(3 - col)
+    to_before.wait_recv()
+    from_after = send_table(4 + col, 4, mate, 4 + col)
+    open_table(4 + col)
     to_after.wait_recv()
     from_before = send_table(col, 3, mate, col)
-    to_before.wait_recv()
-    from_after = send_table(4 + col, 4, mate, 4 + col)
-    to_mate.wait_recv()
+    open_table(col)
+    from_after.wait_recv()
+    open_table(5 - col)
     from_before.wait_recv()
-    from_after.wait_recv()
-
-    def unpack(t, carry):
-        unpack_triangles(table_ref.at[t], full_ref)
-        store_table(t)
-        return carry
-
-    lax.fori_loop(0, 6, unpack, 0)
-
-    for start, count, log_n, offset in PAIRS:
+    open_table(1 - col)
+
+    stores = []
+    for number, (start, count, log_n, offset) in enumerate(PAIRS):
         column_products(start, count, log_n, offset)
-
-    real = valid_ref[...] == 1
-
-    def gather(i, carry):
-        x = o_ref[:, i, :].T
-        x = jnp.concatenate([x[:64], x[64:, :112]], axis=1)
-        out_ref[i] = jnp.where(real, x, 0.0).astype(BF)
-        return carry
-
-    lax.fori_loop(0, 64, gather, 0, unroll=4)
-    store = pltpu.make_async_copy(out_ref, out_hbm, local_sem.at[1])
-    store.start()
+        part = pl.ds(start, count)
+        stores.append(pltpu.make_async_copy(o_ref.at[:, part], out_hbm.at[:, part], local_sem.at[1 + number]))
+        stores[-1].start()
 
     end_round(2)
     for b in range(8):
         grams_ref[:, b, :] = jnp.concatenate([g_ref[b], g_ref[8] if b == 0 else unit], axis=1)
-    store.wait()
+    for copy in stores:
+        copy.wait()
     for copy in (to_after, to_before, to_mate, from_before, from_after):
         copy.wait_send()
     for copy in chain:
         copy.wait_send()
 
 
-def path_kernel(blocks_hbm, grams_ref, out_hbm, path_ref, u_ref, blocks_ref, sem):
-    fetch = pltpu.make_async_copy(blocks_hbm, blocks_ref, sem.at[0])
-    store = pltpu.make_async_copy(blocks_ref, out_hbm, sem.at[1])
-    fetch.start()
-    factor_blocks(grams_ref, u_ref, 0, 4)
-    fetch.wait()
-    store.start()
-    factor_blocks(grams_ref, u_ref, 4, 8)
+def path_kernel(valid_hbm, products_hbm, grams_hbm, out_hbm, path_ref, valid_ref, grams_ref, u_ref, products_ref,
+                out_ref, first_sem, fetch_sem, store_sem):
+    first = (pltpu.make_async_copy(grams_hbm, grams_ref, first_sem.at[0]),
+             pltpu.make_async_copy(valid_hbm, valid_ref, first_sem.at[1]))
+    for copy in first:
+        copy.start()
+
+    def fetch(number):
+        rows = pl.ds(pl.multiple_of(number * 8, 8), 8)
+        return pltpu.make_async_copy(products_hbm.at[rows], products_ref.at[rows], fetch_sem.at[number])
+
+    def store(number):
+        rows = pl.ds(number * 8, 8)
+        return pltpu.make_async_copy(out_ref.at[rows], out_hbm.at[rows], store_sem.at[number])
+
+    def gather(number):
+        for k in range(8):
+            x = products_ref[number * 8 + k].T
+            x = jnp.concatenate([x[:64], x[64:, :112]], axis=1)
+            out_ref[number * 8 + k] = jnp.where(real, x, 0.0).astype(BF)
+
+    for number in range(8):
+        fetch(number).start()
+    for copy in first:
+        copy.wait()
+    real = valid_ref[...] == 1
+    factor_blocks(grams_ref, u_ref, 0, 8, gather,
+                  before=lambda number: fetch(number).wait(), after=lambda number: store(number).start())
     for k in range(9):
         path_ref[0, k] = u_ref[:, k % 8, (k // 8) * 64:(k // 8) * 64 + 64]
-    store.wait()
+    for number in range(8):
+        store(number).wait()
 
 
 def shards(leaf_basis, local_transfer, col_transfer, row_transfer, coupling, slot_block_row, block_col, block_valid):
     blocks = jax.ShapeDtypeStruct((64, 64, 240), BF)
     places = 1 + sum((1 << (high - low)) - 1 for low, high in ROUNDS)
     hbm = pl.BlockSpec(memory_space=pl.ANY)
-    projected, grams = pl.pallas_call(
+    products, grams = pl.pallas_call(
         main_kernel,
-        out_shape=(blocks, jax.ShapeDtypeStruct((64, 8, 128), F32)),
-        in_specs=[SMEM, SMEM, VMEM, VMEM, VMEM, VMEM, hbm, VMEM],
+        out_shape=(jax.ShapeDtypeStruct((64, 128, 128), F32), jax.ShapeDtypeStruct((64, 8, 128), F32)),
+        in_specs=[SMEM, SMEM, VMEM, VMEM, VMEM, VMEM, hbm],
         out_specs=(hbm, VMEM),
         scratch_shapes=[
             pltpu.VMEM((23, 64, 192), BF),
@@ -372,9 +393,8 @@
             pltpu.VMEM((9, 64, 64), F32),
             pltpu.VMEM((64, 64, 240), BF),
             pltpu.VMEM((128, 64, 128), F32),
-            pltpu.VMEM((128, 64, 128), F32),
+            pltpu.VMEM((64, 128, 128), F32),
             pltpu.VMEM((128, 128, 128), BF),
-            pltpu.VMEM((64, 64, 240), BF),
             pltpu.VMEM((6, PACKED, 8, 128), F32),
             pltpu.VMEM((64, 8, 128), F32),
             pltpu.VMEM((16, 64, 128), BF),
@@ -386,26 +406,31 @@
             pltpu.SemaphoreType.DMA((places,)),
             pltpu.SemaphoreType.DMA((5,)),
             pltpu.SemaphoreType.DMA((5,)),
-            pltpu.SemaphoreType.DMA((2,)),
+            pltpu.SemaphoreType.DMA((5,)),
         ],
         compiler_params=pltpu.CompilerParams(
             vmem_limit_bytes=60 * 2**20, collective_id=0, has_side_effects=True),
         name="upsweep_and_projection",
     )(slot_block_row, block_col, leaf_basis.transpose(0, 2, 1), local_transfer, col_transfer[0], row_transfer[0],
-      coupling.transpose(1, 2, 0), block_valid[None])
+      coupling.transpose(1, 2, 0))
     projected, path_factor = pl.pallas_call(
         path_kernel,
         out_shape=(blocks, jax.ShapeDtypeStruct((1, 9, 64, 64), F32)),
-        in_specs=[hbm, VMEM],
+        in_specs=[hbm] * 3,
         out_specs=(hbm, VMEM),
         scratch_shapes=[
+            pltpu.VMEM((1, 240), jnp.int32),
             pltpu.VMEM((64, 8, 128), F32),
+            pltpu.VMEM((64, 8, 128), F32),
+            pltpu.VMEM((64, 128, 128), F32),
             pltpu.VMEM((64, 64, 240), BF),
             pltpu.SemaphoreType.DMA((2,)),
+            pltpu.SemaphoreType.DMA((8,)),
+            pltpu.SemaphoreType.DMA((8,)),
         ],
         compiler_params=pltpu.CompilerParams(vmem_limit_bytes=60 * 2**20),
         name="path_factors",
-    )(projected, grams)
+    )(block_valid[None], products, grams)
     return projected.transpose(2, 0, 1), path_factor
 
 

time: 55.7 us -> 53 us (0.952)
  Pallas kernels: 54.7 us -> 51.6 us
    pallas_call x1, Pallas kernels: 47 us -> 41.7 us  [shards(): pl.pallas_call(main_kernel, out_shape=(jax.ShapeDtypeStruct((64, 128, 128...]
    pallas_call x1, Pallas kernels: 7.71 us -> 9.95 us  [shards(): pl.pallas_call(path_kernel, out_shape=(blocks, jax.ShapeDtypeStruct((1, 9...]
where the time goes in v4:
time: 53 us; the launch traced here: 52.3 us
  Pallas kernels  51.6 us (97%)
  between operations  0.64 us (1%)
    pallas_call x1, Pallas kernels, shards(): pl.pallas_call(main_kernel, out_shape=(jax.ShapeDtypeStruct((64, 128, 128...  41.7 us
    pallas_call x1, Pallas kernels, shards(): pl.pallas_call(path_kernel, out_shape=(blocks, jax.ShapeDtypeStruct((1, 9...  9.95 us

profile of v4, /device:TPU:1, one launch (start us, length us, event | category | flops | bytes accessed | tf_op | source)
XLA Modules:
  0.0 52.3 jit_solution(15241950223130028384)
XLA Ops:
  0.6 41.7 %upsweep_and_projection.1 = (f32[64,128,128]{2,1,0:T(8,128)}, f32[64,8,128]{2,1,0:T(8,128)}) custom-call(s32[240]{0:T(256)} %rows_ref.1, s32[240]{0:T(256)} %cols_ref.1, f32[8,64,128]{2,1,0:T(8,128)} %bitcast.7, bf16[14,64,64]{2,1,0:T(8,128)(2,1)} %local_ref.1, bf16[2,64,64]{2,1,0:T(8,128)(2,1)} %bitcast.9, bf16[8,64,64]{2,1,0:T(8,128)(2,1)} %bitcast.8, ...), custom_call_target="tpu_custom_call" | custom-call | tf_op jit(solution)/shard_map/upsweep_and_projection/pallas_call | solution.py:384
  42.3 10.0 %path_factors.1 = (bf16[64,64,240]{2,1,0:T(8,128)(2,1)}, f32[1,9,64,64]{3,2,1,0:T(8,128)}) custom-call(s32[1,240]{1,0:T(1,128)} %bitcast.10, f32[64,128,128]{2,1,0:T(8,128)} %get-tuple-element.6.products_hbm, f32[64,8,128]{2,1,0:T(8,128)} %get-tuple-element.7.grams_hbm), custom_call_target="tpu_custom_call" | custom-call | tf_op jit(solution)/shard_map/path_factors/pallas_call | solution.py:416

commit v5 on v4

--- a/solution.py
+++ b/solution.py
@@ -250,11 +250,11 @@
             later = jnp.concatenate([x[:, 128:], pad], axis=1)
             t_ref[:, number * 8 + k, :] = jnp.concatenate([x[:, :128], later], axis=0).T
 
-    factor_blocks(a_ref, u_ref, 0, 3, spread)
+    factor_blocks(a_ref, u_ref, 0, 2, spread)
     chain[0].wait_recv()
     g_ref[0] = unfolded(out_buf[0] + in_buf[0])
     send_round(0)
-    factor_blocks(a_ref, u_ref, 3, 8, spread)
+    factor_blocks(a_ref, u_ref, 2, 8, spread)
     mine = 2 + col
     pack_triangles(u_ref, table_ref.at[mine])
     to_after = send_table(mine, 0, (after, col), col)

time: 53 us -> 53.3 us (level)
  no operation moved by 1% of the time
where the time goes in v5:
time: 53.3 us; the launch traced here: 52.4 us
  Pallas kernels  51.7 us (97%)
  between operations  0.64 us (1%)
    pallas_call x1, Pallas kernels, shards(): pl.pallas_call(main_kernel, out_shape=(jax.ShapeDtypeStruct((64, 128, 128...  41.8 us
    pallas_call x1, Pallas kernels, shards(): pl.pallas_call(path_kernel, out_shape=(blocks, jax.ShapeDtypeStruct((1, 9...  9.95 us

profile of v5, /device:TPU:1, one launch (start us, length us, event | category | flops | bytes accessed | tf_op | source)
XLA Modules:
  0.0 52.4 jit_solution(6192491663840831142)
XLA Ops:
  0.6 41.8 %upsweep_and_projection.1 = (f32[64,128,128]{2,1,0:T(8,128)}, f32[64,8,128]{2,1,0:T(8,128)}) custom-call(s32[240]{0:T(256)} %rows_ref.1, s32[240]{0:T(256)} %cols_ref.1, f32[8,64,128]{2,1,0:T(8,128)} %bitcast.7, bf16[14,64,64]{2,1,0:T(8,128)(2,1)} %local_ref.1, bf16[2,64,64]{2,1,0:T(8,128)(2,1)} %bitcast.9, bf16[8,64,64]{2,1,0:T(8,128)(2,1)} %bitcast.8, ...), custom_call_target="tpu_custom_call" | custom-call | tf_op jit(solution)/shard_map/upsweep_and_projection/pallas_call | solution.py:384
  42.4 10.0 %path_factors.1 = (bf16[64,64,240]{2,1,0:T(8,128)(2,1)}, f32[1,9,64,64]{3,2,1,0:T(8,128)}) custom-call(s32[1,240]{1,0:T(1,128)} %bitcast.10, f32[64,128,128]{2,1,0:T(8,128)} %get-tuple-element.6.products_hbm, f32[64,8,128]{2,1,0:T(8,128)} %get-tuple-element.7.grams_hbm), custom_call_target="tpu_custom_call" | custom-call | tf_op jit(solution)/shard_map/path_factors/pallas_call | solution.py:416
